TPU v7x, 32 devices: a whole 2x2x4 slice. The times are simulated.
32 devices in a mesh: pair: 8 (over z, x), win: 4 (over y, core).
Axes of the slice: x: 2, y: 2, z: 4, core: 2. Of those that a mesh axis runs over, the one named last changes fastest.
Arguments:
- spectra: bfloat16 [32, 2, 384, 2048], P(None, None, 'win', 'pair'), may hold values from -6 to 6
- channel_order: int32 [8, 256], P('pair'), may hold values from 0 to 255, each once within a row
- partners: int32 [4, 8], replicated, may hold values from 0 to 7, as said below
Outputs:
- stacks: float32 [8, 256, 4, 16, 256], P('pair', 'win')
Inputs may be any that keep to these rules, and one draw needn't show every extreme that they name: For every round r and block b, partners[r, b] differs from b and partners[r, partners[r, b]] = b; no two rounds match the same two blocks. `channel_order`: each row lists every slot once.
All inputs are finite; a program needn't handle non-finite values.
Results may differ from a plain program's by a relative error of at most 0.004.
Values may be sent and summed in bfloat16 or wider, within the bound.
A program may use at most 128 MiB of HBM per device.

v0:
```python
import math

import jax
import jax.numpy as jnp
from jax import lax
from jax.sharding import PartitionSpec as P

LAGS = 16
ROUNDS = 4


def whiten(spectra):
    values = spectra.astype(jnp.float32)
    band_power = values[:, 0] * values[:, 0] + values[:, 1] * values[:, 1]
    num_bins = band_power.shape[0]
    padded = jnp.pad(band_power, ((2, 2), (0, 0), (0, 0)))
    band_total = (
        padded[0:num_bins]
        + padded[1 : num_bins + 1]
        + padded[2 : num_bins + 2]
        + padded[3 : num_bins + 3]
        + padded[4 : num_bins + 4]
    )
    bin_index = jnp.arange(num_bins, dtype=jnp.int32)
    counts = (jnp.minimum(bin_index + 2, num_bins - 1) - jnp.maximum(bin_index - 2, 0) + 1).astype(
        jnp.float32
    )
    band_mean = band_total / counts[:, None, None]
    inv_scale = 1.0 / jnp.maximum(jnp.sqrt(band_mean), 0.5)
    return (values * inv_scale[:, None]).astype(jnp.bfloat16)


def make_table(num_bins, num_lags, window_total):
    bin_freq = jnp.arange(num_bins, dtype=jnp.float32)[:, None]
    lag_index = (jnp.arange(num_lags, dtype=jnp.int32) - num_lags // 2).astype(jnp.float32)[None, :]
    phase_angle = math.pi * bin_freq * lag_index / num_bins
    norm_factor = 1.0 / math.sqrt(window_total * num_bins)
    return jnp.concatenate([jnp.cos(phase_angle), -jnp.sin(phase_angle)], 0) * norm_factor


def prepare(mate_block):
    num_bins, _, num_windows, num_cols = mate_block.shape
    right_real = mate_block.reshape(num_bins, 2 * num_windows, num_cols)
    right_turned = jnp.concatenate([mate_block[:, 1], -mate_block[:, 0]], axis=1)
    return (right_real, right_turned)


def correlate(own_block, mate_pair, lag_table, row_count):
    num_bins, _, num_windows, _ = own_block.shape
    left_rows = own_block.reshape(num_bins, 2 * num_windows, row_count)
    cross_real = jnp.einsum(
        "fki,fkj->fij", left_rows, mate_pair[0], preferred_element_type=jnp.float32
    )
    cross_imag = jnp.einsum(
        "fki,fkj->fij", left_rows, mate_pair[1], preferred_element_type=jnp.float32
    )
    stacked = jnp.concatenate([cross_real, cross_imag], 0)
    return jnp.einsum("gl,gij->ilj", lag_table, stacked, precision=lax.Precision.HIGHEST)


def local(spectra, channel_order, partners):
    whitened = whiten(spectra)
    own_block = jnp.take(whitened, channel_order[0], axis=3)
    num_blocks = lax.axis_size("pair")
    win_count = lax.axis_size("win")
    window_total = spectra.shape[2] * win_count
    lag_table = make_table(spectra.shape[0], LAGS, window_total)
    own_pieces = own_block.reshape(num_blocks, -1)
    share_rows = own_block.shape[3] // win_count
    turned = lax.all_to_all(own_pieces, "pair", split_axis=0, concat_axis=0, tiled=True)
    results = []
    for turn_index in range(ROUNDS):
        arranged = jnp.take(turned, partners[turn_index], axis=0)
        received = lax.all_to_all(arranged, "pair", split_axis=0, concat_axis=0, tiled=True)
        mate_pair = prepare(received.reshape(own_block.shape))

        def term_rows(first_row, row_count, mate_pair=mate_pair):
            return correlate(own_block, mate_pair, lag_table, row_count)

        results.append(
            lax.psum_scatter(
                term_rows(jnp.int32(0), share_rows * lax.axis_size("win")),
                "win",
                scatter_dimension=0,
                tiled=True,
            )
        )
    stacks = jnp.stack(results, 1)
    return stacks[None]


def solution(mesh):
    return jax.shard_map(
        local,
        mesh=mesh,
        in_specs=(P(None, None, "win", "pair"), P("pair", None), P()),
        out_specs=P("pair", "win", None, None, None),
        check_vma=False,
    )
```

profile of v0, /device:TPU:0, one launch (start us, length us, event | category | flops | bytes accessed | tf_op | source)
XLA Modules:
  0.0 646.6 jit_solution(13733863401749289330)
XLA Ops:
  6.5 7.6 %copy.60 = bf16[32,2,96,256]{2,0,3,1:T(8,128)(2,1)} copy(bf16[32,2,96,256]{3,2,1,0:T(8,128)(2,1)} %param.5) | data formatting | bytes 6291456 | tf_op args[0]
  14.2 3.4 convert_element_type.24
  18.6 3.5 maximum_divide_fusion
  22.1 3.0 multiply_convert_fusion
  25.1 5.2 gather_fusion
  30.3 4.0 broadcast_select_fusion
  34.4 5.8 copy.62
  40.2 4.5 select_n.60
  45.3 19.5 %reduce.8 = bf16[8,196608]{1,0:T(8,128)(2,1)S(1)} reduce(bf16[8,1,196608]{2,1,0:T(2,128)(2,1)} %select_n.60, bf16[]{:T(256)} %broadcast.180), dimensions={1}, to_apply=%select_n.60.reduce_sub_computation | reduce | bytes 6291458 | tf_op jit(solution)/shard_map/jit(_take)/select_n | solution.py:63
  64.7 4.5 reshape.234
  69.3 7.6 %all-to-all-start = ((bf16[8,2,98304]{2,1,0:T(2,128)(2,1)}), bf16[8,2,98304]{2,1,0:T(2,128)(2,1)S(1)}, u32[]{:S(2)}, u32[]{:S(2)}) async-start(bf16[8,2,98304]{2,1,0:T(2,128)(2,1)} %reshape.234), calls=%async_computation | async-start | bytes 6291456 | tf_op jit(solution)/shard_map/all_to_all | solution.py:70
  77.0 70.6 %all-to-all-done = bf16[8,2,98304]{2,1,0:T(2,128)(2,1)S(1)} async-done(((bf16[8,2,98304]{2,1,0:T(2,128)(2,1)}), bf16[8,2,98304]{2,1,0:T(2,128)(2,1)S(1)}, u32[]{:S(2)}, u32[]{:S(2)}) %all-to-all-start) | async-done | bytes 3145760 | tf_op jit(solution)/shard_map/all_to_all | solution.py:70
  147.6 5.3 reshape.235
  152.9 6.8 %copy.107 = bf16[8,1,196608]{2,0,1:T(8,128)(2,1)S(1)} copy(bf16[8,1,196608]{2,1,0:T(2,128)(2,1)} %reshape.235) | data formatting | bytes 6291456
  159.9 2.8 gather_fusion.2
  165.5 2.8 gather_fusion.3
  171.1 7.1 %fusion.16 = (bf16[8,1,196608]{2,0,1:T(8,128)(2,1)}, bf16[8,1,196608]{2,0,1:T(8,128)(2,1)}) fusion(bf16[8,98304]{1,0:T(8,128)(2,1)} %gather_fusion.2, bf16[8,98304]{1,0:T(8,128)(2,1)} %gather_fusion.1, pred[8]{0:T(512)(128)(4,1)S(1)} %get-tuple-element.6, bf16[8,98304]{1,0:T(8,128)(2,1)} %gather_fusion.4, bf16[8,98304]{1,0:T(8,128)(2,1)} %gather_fusion.3, ...), kind=kLoop, calls=%fused_computation.40 | loop fusion | flops 15728640 | bytes 12582928 | tf_op jit(solution)/shard_map/all_to_all | solution.py:74
  178.1 5.7 reduce.12
  183.8 6.4 reshape.242
  190.2 4.5 all-to-all-start.1
  194.7 7.2 %copy.61 = bf16[32,2,96,256]{3,2,1,0:T(8,128)(2,1)} copy(bf16[32,2,96,256]{2,0,1,3:T(8,128)(2,1)} %bitcast.115) | data formatting | bytes 6291456 | tf_op jit(solution)/shard_map/jit(_take)/gather | solution.py:63
  202.2 3.8 bitcast_select_fusion
  217.1 3.6 reduce.11
  220.7 4.6 reshape.240
  225.3 39.6 %all-to-all-done.1 = bf16[8,2,98304]{2,1,0:T(2,128)(2,1)} async-done(((bf16[8,2,98304]{2,1,0:T(2,128)(2,1)}), bf16[8,2,98304]{2,1,0:T(2,128)(2,1)}, u32[]{:S(2)}, u32[]{:S(2)}) %all-to-all-start.1) | async-done | bytes 3145760 | tf_op jit(solution)/shard_map/all_to_all | solution.py:74
  264.9 4.5 all-to-all-start.2
  269.4 7.9 %reshape.243 = bf16[8,1,196608]{2,1,0:T(2,128)(2,1)} reshape(bf16[8,2,98304]{2,1,0:T(2,128)(2,1)} %all-to-all-done.1) | data formatting | bytes 6291456
  277.3 18.8 %reduce = bf16[8,196608]{1,0:T(8,128)(2,1)S(1)} reduce(bf16[8,1,196608]{2,1,0:T(2,128)(2,1)} %reshape.243, bf16[]{:T(256)} %constant.55), dimensions={1}, to_apply=%all_to_all.33.reduce_sub_computation | reduce | bytes 6291458 | tf_op jit(solution)/shard_map/all_to_all | solution.py:74
  296.2 3.1 reshape.125
  299.2 2.8 fusion.55
  303.4 5.1 reshape_reshape.12
  308.5 3.4 fusion.68
  311.9 4.7 fusion.17
  316.5 4.8 pad_maximum_fusion
  321.3 16.6 %fusion.36 = f32[256,16,256]{2,1,0:T(8,128)} fusion(f32[64,16,1]{0,1,2:T(8,128)S(1)} %fusion.56, f32[64,256,256]{2,1,0:T(8,128)S(1)} %pad_maximum_fusion), kind=kOutput, calls=%fused_computation.65 | convolution fusion | flops 805306368 | bytes 20975616 | tf_op jit(solution)/shard_map/gl,gij->ilj/dot_general | solution.py:58
  337.9 7.0 %fusion.26 = (bf16[8,1,196608]{2,0,1:T(8,128)(2,1)}, bf16[8,1,196608]{2,0,1:T(8,128)(2,1)}) fusion(bf16[8,98304]{1,0:T(8,128)(2,1)} %gather_fusion.6, bf16[8,98304]{1,0:T(8,128)(2,1)} %gather_fusion.5, pred[8]{0:T(512)(128)(4,1)S(1)} %get-tuple-element.20, bf16[8,98304]{1,0:T(8,128)(2,1)} %gather_fusion.8, bf16[8,98304]{1,0:T(8,128)(2,1)} %gather_fusion.7, ...), kind=kLoop, calls=%fused_computation.52 | loop fusion | flops 15728640 | bytes 12582928 | tf_op jit(solution)/shard_map/all_to_all | solution.py:74
  344.9 6.3 reduce.10
  351.2 6.4 reshape.238
  357.6 6.0 all-to-all-start.3
  363.7 7.7 %reshape.241 = bf16[8,1,196608]{2,1,0:T(2,128)(2,1)} reshape(bf16[8,2,98304]{2,1,0:T(2,128)(2,1)} %all-to-all-done.2) | data formatting | bytes 6291456
  371.4 20.5 %reduce.2 = bf16[8,196608]{1,0:T(8,128)(2,1)} reduce(bf16[8,1,196608]{2,1,0:T(2,128)(2,1)} %reshape.241, bf16[]{:T(256)} %constant.55), dimensions={1}, to_apply=%all_to_all.35.reduce_sub_computation | reduce | bytes 6291458 | tf_op jit(solution)/shard_map/all_to_all | solution.py:74
  391.9 5.0 reshape.126
  396.9 5.0 reshape_reshape.13
  406.2 4.6 fusion.69
  410.8 4.8 pad_maximum_fusion.1
  415.7 16.5 %fusion.39 = f32[256,16,256]{2,1,0:T(8,128)} fusion(f32[64,16,1]{0,1,2:T(8,128)S(1)} %fusion.56, f32[64,256,256]{2,1,0:T(8,128)S(1)} %pad_maximum_fusion.1), kind=kOutput, calls=%fused_computation.66 | convolution fusion | flops 805306368 | bytes 20975616 | tf_op jit(solution)/shard_map/gl,gij->ilj/dot_general | solution.py:58
  432.3 5.3 reduce.9
  437.5 6.7 %reshape.236 = bf16[8,2,98304]{2,1,0:T(2,128)(2,1)} reshape(bf16[8,196608]{1,0:T(8,128)(2,1)} %reduce.9) | data formatting | bytes 6291456
  444.2 6.4 all-to-all-start.4
  450.6 7.8 %reshape.239 = bf16[8,1,196608]{2,1,0:T(2,128)(2,1)} reshape(bf16[8,2,98304]{2,1,0:T(2,128)(2,1)} %all-to-all-done.3) | data formatting | bytes 6291456
  458.4 20.5 %reduce.4 = bf16[8,196608]{1,0:T(8,128)(2,1)} reduce(bf16[8,1,196608]{2,1,0:T(2,128)(2,1)} %reshape.239, bf16[]{:T(256)} %constant.55), dimensions={1}, to_apply=%all_to_all.37.reduce_sub_computation | reduce | bytes 6291458 | tf_op jit(solution)/shard_map/all_to_all | solution.py:74
  478.9 5.1 reshape.127
  484.0 5.0 reshape_reshape.14
  493.4 4.7 fusion.70
  498.0 4.8 pad_maximum_fusion.2
  502.9 16.8 %fusion.42 = f32[256,16,256]{2,1,0:T(8,128)} fusion(f32[64,16,1]{0,1,2:T(8,128)S(1)} %fusion.56, f32[64,256,256]{2,1,0:T(8,128)S(1)} %pad_maximum_fusion.2), kind=kOutput, calls=%fused_computation.67 | convolution fusion | flops 805306368 | bytes 20975616 | tf_op jit(solution)/shard_map/gl,gij->ilj/dot_general | solution.py:58
  519.7 8.1 %reshape.237 = bf16[8,1,196608]{2,1,0:T(2,128)(2,1)} reshape(bf16[8,2,98304]{2,1,0:T(2,128)(2,1)} %all-to-all-done.4) | data formatting | bytes 6291456
  527.8 20.6 %reduce.6 = bf16[8,196608]{1,0:T(8,128)(2,1)} reduce(bf16[8,1,196608]{2,1,0:T(2,128)(2,1)} %reshape.237, bf16[]{:T(256)} %constant.55), dimensions={1}, to_apply=%all_to_all.39.reduce_sub_computation | reduce | bytes 6291458 | tf_op jit(solution)/shard_map/all_to_all | solution.py:74
  548.5 5.0 reshape.128
  553.4 5.1 reshape_reshape.15
  563.0 4.6 fusion.71
  567.6 4.8 pad_maximum_fusion.3
  572.4 16.5 %fusion.45 = f32[256,16,256]{2,1,0:T(8,128)} fusion(f32[64,16,1]{0,1,2:T(8,128)S(1)} %fusion.56, f32[64,256,256]{2,1,0:T(8,128)S(1)} %pad_maximum_fusion.3), kind=kOutput, calls=%fused_computation.68 | convolution fusion | flops 805306368 | bytes 20975616 | tf_op jit(solution)/shard_map/gl,gij->ilj/dot_general | solution.py:58
  589.1 45.5 %reduce-scatter.11.cloned.1.call-done = f32[64,16,256]{2,1,0:T(8,128)} async-done(((f32[256,16,256]{2,1,0:T(8,128)}), f32[64,16,256]{2,1,0:T(8,128)}) %reduce-scatter.11.cloned.1.call-update) | async-done | bytes 1048592 | tf_op jit(solution)/shard_map/reduce_scatter | solution.py:81
  (76 shorter events, 38.7 us)
Async XLA Ops:
  18.6 3.5 copy-start.1
  22.1 3.0 copy-start.13
  69.3 7.6 %copy-start.12 = (s32[4,8]{1,0:T(4,128)S(1)}, s32[4,8]{1,0:T(4,128)}, u32[]{:S(2)}) copy-start(s32[4,8]{1,0:T(4,128)} %param.7) | copy-start | bytes 388
  69.3 78.3 %all-to-all-start = ((bf16[8,2,98304]{2,1,0:T(2,128)(2,1)}), bf16[8,2,98304]{2,1,0:T(2,128)(2,1)S(1)}, u32[]{:S(2)}, u32[]{:S(2)}) async-start(bf16[8,2,98304]{2,1,0:T(2,128)(2,1)} %reshape.234), calls=%async_computation | async-start | bytes 6291456 | tf_op jit(solution)/shard_map/all_to_all | solution.py:70
  190.2 74.7 %all-to-all-start.1 = ((bf16[8,2,98304]{2,1,0:T(2,128)(2,1)}), bf16[8,2,98304]{2,1,0:T(2,128)(2,1)}, u32[]{:S(2)}, u32[]{:S(2)}) async-start(bf16[8,2,98304]{2,1,0:T(2,128)(2,1)} %reshape.242), calls=%async_computation.1 | async-start | bytes 6291456 | tf_op jit(solution)/shard_map/all_to_all | solution.py:74
  264.9 92.7 %all-to-all-start.2 = ((bf16[8,2,98304]{2,1,0:T(2,128)(2,1)}), bf16[8,2,98304]{2,1,0:T(2,128)(2,1)}, u32[]{:S(2)}, u32[]{:S(2)}) async-start(bf16[8,2,98304]{2,1,0:T(2,128)(2,1)} %reshape.240), calls=%async_computation.3 | async-start | bytes 6291456 | tf_op jit(solution)/shard_map/all_to_all | solution.py:74
  269.4 319.6 %reduce-scatter.5.cloned.1.call-start = ((), (), s32[]{:S(2)}) async-start(), calls=%async_computation.9 | async-start | bytes 5242880 | tf_op jit(solution)/shard_map/reduce_scatter | solution.py:81
  296.1 3.1 copy-start.2
  299.2 2.8 copy-start.9
  303.4 5.1 copy-start
  308.5 3.4 copy-start.10
  308.5 3.4 copy-start.11
  357.6 86.5 %all-to-all-start.3 = ((bf16[8,2,98304]{2,1,0:T(2,128)(2,1)}), bf16[8,2,98304]{2,1,0:T(2,128)(2,1)}, u32[]{:S(2)}, u32[]{:S(2)}) async-start(bf16[8,2,98304]{2,1,0:T(2,128)(2,1)} %reshape.238), calls=%async_computation.5 | async-start | bytes 6291456 | tf_op jit(solution)/shard_map/all_to_all | solution.py:74
  363.6 225.4 %reduce-scatter.7.cloned.1.call-start = ((), (), s32[]{:S(2)}) async-start(), calls=%async_computation.10 | async-start | bytes 5242880 | tf_op jit(solution)/shard_map/reduce_scatter | solution.py:81
  401.8 2.4 copy-start.6
  404.3 1.9 copy-start.4
  444.2 75.5 %all-to-all-start.4 = ((bf16[8,2,98304]{2,1,0:T(2,128)(2,1)}), bf16[8,2,98304]{2,1,0:T(2,128)(2,1)}, u32[]{:S(2)}, u32[]{:S(2)}) async-start(bf16[8,2,98304]{2,1,0:T(2,128)(2,1)} %reshape.236), calls=%async_computation.7 | async-start | bytes 6291456 | tf_op jit(solution)/shard_map/all_to_all | solution.py:74
  450.6 138.5 %reduce-scatter.9.cloned.1.call-start = ((), (), s32[]{:S(2)}) async-start(), calls=%async_computation.11 | async-start | bytes 5242880 | tf_op jit(solution)/shard_map/reduce_scatter | solution.py:81
  489.0 2.4 copy-start.7
  491.5 1.9 copy-start.5
  519.7 114.9 %reduce-scatter.11.cloned.1.call-start = ((), (), s32[]{:S(2)}) async-start(), calls=%async_computation.12 | async-start | bytes 5242880 | tf_op jit(solution)/shard_map/reduce_scatter | solution.py:81
  558.5 2.5 copy-start.8
  561.1 1.9 copy-start.3
Sparse Core Ops, SparseCore 0:
  338.0 45.8 reduce-scatter.4
  432.4 45.9 reduce-scatter.6
  519.8 45.6 reduce-scatter.8
  589.1 45.4 reduce-scatter.10
where the time goes:
time: 657 us; the launch traced here: 647 us
  other arithmetic  184 us (28%)
  local copies, waits for them, and re-layouts  172 us (26%)
  waiting for transfers between devices  156 us (24%)
  matrix products  92.3 us (14%)
  starting transfers between devices  29 us (4%)
  between operations  13.7 us (2%)
    all_to_all x10, other arithmetic, local(): lax.all_to_all(arranged, 'pair', split_axis=0, concat_axis=0, tiled=True)  115 us
    unnamed x40, local copies, waits for them, and re-layouts  83.8 us
    all_to_all x1, waiting for transfers between devices, local(): lax.all_to_all(own_pieces, 'pair', split_axis=0, concat_axis=0, tiled=True)  70.6 us
    dot_general x4, matrix products, correlate(): jnp.einsum('gl,gij->ilj', lag_table, stacked, precision=lax.Precision.HIG...  66.4 us
    reduce_scatter x4, waiting for transfers between devices, local(): lax.psum_scatter(term_rows(jnp.int32(0), share_rows * lax.axis_size('win'...  45.6 us
    all_to_all x4, waiting for transfers between devices, local(): lax.all_to_all(arranged, 'pair', split_axis=0, concat_axis=0, tiled=True)  39.6 us
    select_n x4, other arithmetic, local(): own_block = jnp.take(whitened, channel_order[0], axis=3)  27.4 us
    gather x9, local copies, waits for them, and re-layouts, local(): arranged = jnp.take(turned, partners[turn_index], axis=0)  22.4 us
  transfers between devices with their start and end apart: 9, of which 3 were waited for; matrix products, arithmetic and copies ran while one was open for 52% of the time, Pallas kernels for 0%

commit v1 on v0

v1 whole, which is shorter than its diff:
```python
import functools
import math

import jax
import jax.numpy as jnp
from jax import lax
from jax.experimental import pallas as pl
from jax.experimental.pallas import tpu as pltpu
from jax.sharding import PartitionSpec as P

LAGS = 16
ROUNDS = 4
GROUP = 16
BF = jnp.bfloat16
F32 = jnp.float32


def make_table(num_bins, num_lags, window_total):
    bin_freq = jnp.arange(num_bins, dtype=F32)[:, None]
    lag_index = (jnp.arange(num_lags, dtype=jnp.int32) - num_lags // 2).astype(F32)[None, :]
    phase_angle = math.pi * bin_freq * lag_index / num_bins
    norm_factor = 1.0 / math.sqrt(window_total * num_bins)
    return jnp.concatenate([jnp.cos(phase_angle), -jnp.sin(phase_angle)], 0) * norm_factor


def whiten_kernel(spec_ref, order_ref, own_ref, lhs_ref, power):
    nf, _, nw, nc = spec_ref.shape
    zero = jnp.zeros((nw, nc), F32)
    for edge in (0, 1, nf + 2, nf + 3):
        power[edge] = zero

    def square(f, carry):
        re = spec_ref[f, 0].astype(F32)
        im = spec_ref[f, 1].astype(F32)
        power[f + 2] = re * re + im * im
        return carry

    lax.fori_loop(0, nf, square, 0)
    rows = lax.broadcasted_iota(jnp.int32, (nc, nc), 0)
    cols = lax.broadcasted_iota(jnp.int32, (nc, nc), 1)
    pick = (rows == order_ref[...]).astype(F32).astype(BF)
    eye = (rows == cols).astype(F32).astype(BF)

    def scale(f, carry):
        total = power[f] + power[f + 1] + power[f + 2] + power[f + 3] + power[f + 4]
        count = jnp.minimum(f + 2, nf - 1) - jnp.maximum(f - 2, 0) + 1
        mean = total / count.astype(F32)
        inv = 1.0 / jnp.maximum(jnp.sqrt(mean), 0.5)
        white = jnp.concatenate(
            [
                (spec_ref[f, 0].astype(F32) * inv).astype(BF),
                (spec_ref[f, 1].astype(F32) * inv).astype(BF),
            ],
            0,
        )
        own = jnp.dot(white, pick, preferred_element_type=F32).astype(BF)
        own_ref[f] = own
        turned = lax.dot_general(eye, own, (((1,), (1,)), ((), ())), preferred_element_type=F32)
        lhs_ref[f] = turned.astype(BF)
        return carry

    lax.fori_loop(0, nf, scale, 0)


def whiten(spectra, order):
    nf, _, nw, nc = spectra.shape
    vmem = pl.BlockSpec(memory_space=pltpu.VMEM)
    return pl.pallas_call(
        whiten_kernel,
        out_shape=(
            jax.ShapeDtypeStruct((nf, 2 * nw, nc), BF),
            jax.ShapeDtypeStruct((nf, nc, 2 * nw), BF),
        ),
        in_specs=[vmem, vmem],
        out_specs=(vmem, vmem),
        scratch_shapes=[pltpu.VMEM((nf + 4, nw, nc), F32)],
        compiler_params=pltpu.CompilerParams(vmem_limit_bytes=40 * 2**20),
        name="whiten",
    )(spectra, order)


def corr_kernel(info_ref, lhs_ref, table_ref, *refs):
    mates = refs[:-5]
    keep_ref, send_ref, mate, cross, sem = refs[-5:]
    nf, nk, nc = mate.shape
    nw = nk // 2
    slot, core, row = info_ref[0], info_ref[1], info_ref[2]
    for s, ref in enumerate(mates):

        @pl.when(slot == s)
        def _(ref=ref):
            pltpu.make_async_copy(ref, mate, sem).start()

    pltpu.make_async_copy(mates[0], mate, sem).wait()

    def one_bin(f, carry):
        right = mate[f]
        turned = jnp.concatenate([right[nw:], -right[:nw]], 0)
        left = lhs_ref[f]
        cross[f] = jnp.dot(left, right, preferred_element_type=F32).astype(BF)
        cross[nf + f] = jnp.dot(left, turned, preferred_element_type=F32).astype(BF)
        return carry

    lax.fori_loop(0, nf, one_bin, 0)
    share = keep_ref.shape[1]
    per = share // GROUP

    def one_group(step, carry):
        half, u = step // per, step % per
        for other, out_ref in ((0, keep_ref), (1, send_ref)):
            owner = lax.rem(row + half, 2) * 2 + lax.rem(core + other, 2)
            start = pl.multiple_of(owner * share + u * GROUP, GROUP)
            right = cross[:, pl.ds(start, GROUP), :].reshape(2 * nf * GROUP, nc)
            lags = jnp.dot(table_ref[...], right, preferred_element_type=F32)
            at = pl.multiple_of(u * GROUP, GROUP)
            out_ref[half, pl.ds(at, GROUP)] = lags.reshape(GROUP, LAGS, nc).astype(out_ref.dtype)
        return carry

    lax.fori_loop(0, 2 * per, one_group, 0)


def correlate(info, lhs, table, mates):
    nf, nc, nk = lhs.shape
    vmem = pl.BlockSpec(memory_space=pltpu.VMEM)
    return pl.pallas_call(
        corr_kernel,
        out_shape=(
            jax.ShapeDtypeStruct((2, nc // 4, LAGS, nc), F32),
            jax.ShapeDtypeStruct((2, nc // 4, LAGS, nc), BF),
        ),
        in_specs=[pl.BlockSpec(memory_space=pltpu.SMEM), vmem, vmem]
        + [pl.BlockSpec(memory_space=pl.ANY)] * len(mates),
        out_specs=(vmem, vmem),
        scratch_shapes=[
            pltpu.VMEM((nf, nk, nc), BF),
            pltpu.VMEM((2 * nf, nc, nc), BF),
            pltpu.SemaphoreType.DMA,
        ],
        cost_estimate=pl.CostEstimate(
            flops=8_000_000_000, bytes_accessed=12_000_000, transcendentals=0
        ),
        compiler_params=pltpu.CompilerParams(vmem_limit_bytes=40 * 2**20),
        name="correlate",
    )(info, lhs, table, *mates)


def gather_blocks(own, blocks):
    chain = blocks // 2
    got = {}

    def send(block, pairs):
        return lax.ppermute(block, "pair", pairs)

    def chain_pairs(step, depth):
        links = []
        for c in range(chain):
            src = c + step
            if 0 <= c + step * depth < chain:
                links += [(2 * src + x, 2 * c + x) for x in range(2)]
        return links

    def swap_pairs(reach):
        return [
            (2 * c + x, 2 * c + 1 - x)
            for c in range(chain)
            if 0 <= c + reach < chain
            for x in range(2)
        ]

    got[(0, 1)] = send(own, swap_pairs(0))
    for depth in range(1, chain):
        for step in (1, -1):
            before = own if depth == 1 else got[(step * (depth - 1), 0)]
            got[(step * depth, 0)] = send(before, chain_pairs(step, depth))
    for depth in range(1, chain):
        for step in (1, -1):
            got[(step * depth, 1)] = send(got[(step * depth, 0)], swap_pairs(step * depth))
    return got


ARRIVAL = [(0, 1), (1, 0), (-1, 0), (2, 0), (-2, 0), (1, 1), (-1, 1)]
ARRIVAL += [(3, 0), (-3, 0), (2, 1), (-2, 1), (3, 1), (-3, 1)]
READY = (7, 9, 11, 13)


def local(spectra, channel_order, partners):
    num_blocks = lax.axis_size("pair")
    win_count = lax.axis_size("win")
    nf, _, nw, nc = spectra.shape
    table = make_table(nf, LAGS, nw * win_count)
    spread = (
        table.T[None, :, :, None] * jnp.eye(GROUP, dtype=F32)[:, None, None, :]
    ).reshape(GROUP * LAGS, 2 * nf * GROUP).astype(BF)
    own, lhs = whiten(spectra, channel_order)
    me = lax.axis_index("pair")
    win = lax.axis_index("win")
    row, core = win // 2, win % 2
    mine = partners[:, me]
    results = []
    if num_blocks == 8:
        got = gather_blocks(own, num_blocks)
        reach = mine // 2 - me // 2
        column = jnp.abs(mine % 2 - me % 2)
        rank = jnp.zeros_like(mine)
        for index, (step, other) in enumerate(ARRIVAL):
            rank = jnp.where((reach == step) & (column == other), index, rank)
        place = jnp.sum((rank[None, :] < rank[:, None]).astype(jnp.int32), 1)
    else:
        place = None
        turned = lax.all_to_all(
            own.reshape(num_blocks, -1), "pair", split_axis=0, concat_axis=0, tiled=True
        )
    for turn in range(ROUNDS):
        if place is None:
            arranged = jnp.take(turned, partners[turn], axis=0)
            received = lax.all_to_all(arranged, "pair", split_axis=0, concat_axis=0, tiled=True)
            mates, slot = [received.reshape(own.shape)], jnp.int32(0)
        else:
            mates = [got[key] for key in ARRIVAL[: READY[turn]]]
            slot = jnp.sum(jnp.where(place == turn, rank, 0))
        info = jnp.stack([slot, core, row]).astype(jnp.int32)
        keep, give = correlate(info, lhs, spread, mates)
        beside = lax.ppermute(give, "win", [(w, w ^ 1) for w in range(win_count)])
        passed = (keep[1] + beside[1].astype(F32)).astype(BF)
        across = lax.ppermute(passed, "win", [(w, w ^ 2) for w in range(win_count)])
        results.append(keep[0] + beside[0].astype(F32) + across.astype(F32))
    if place is None:
        return jnp.stack(results, 1)[None]
    ordered = []
    for turn in range(ROUNDS):
        at = place[turn]
        value = results[ROUNDS - 1]
        for k in range(ROUNDS - 1):
            value = jnp.where(at == k, results[k], value)
        ordered.append(value)
    return jnp.stack(ordered, 1)[None]


def solution(mesh):
    return jax.shard_map(
        local,
        mesh=mesh,
        in_specs=(P(None, None, "win", "pair"), P("pair", None), P()),
        out_specs=P("pair", "win", None, None, None),
        check_vma=False,
    )
```

time: 657 us -> 470 us (0.72)
  the two profiles are of different devices: /device:TPU:0 before, /device:TPU:22 now
where the time goes in v1:
time: 470 us; the launch traced here: 469 us
  waiting for transfers between devices  310 us (66%)
  Pallas kernels  73.5 us (16%)
  starting transfers between devices  44.3 us (9%)
  local copies, waits for them, and re-layouts  23.1 us (5%)
  other arithmetic  10 us (2%)
  between operations  8.11 us (2%)
    ppermute x13, waiting for transfers between devices, send(): return lax.ppermute(block, 'pair', pairs)  276 us
    pallas_call x4, Pallas kernels, correlate(): pl.pallas_call(corr_kernel, out_shape=(jax.ShapeDtypeStruct((2, nc // 4,...  59.9 us
    ppermute x13, starting transfers between devices, send(): return lax.ppermute(block, 'pair', pairs)  39.2 us
    ppermute x4, waiting for transfers between devices, local(): across = lax.ppermute(passed, 'win', [(w, w ^ 2) for w in range(win_count)])  34.4 us
    pallas_call x1, Pallas kernels, whiten(): pl.pallas_call(whiten_kernel, out_shape=(jax.ShapeDtypeStruct((nf, 2 * nw...  13.6 us
    unnamed x20, local copies, waits for them, and re-layouts  10.9 us
  transfers between devices with their start and end apart: 21, of which 9 were waited for; matrix products, arithmetic and copies ran while one was open for 4% of the time, Pallas kernels for 13%

profile of v1, /device:TPU:22, one launch (start us, length us, event | category | flops | bytes accessed | tf_op | source)
XLA Modules:
  0.0 468.9 jit_solution(3130798496940358125)
XLA Ops:
  0.0 1.9 copy-done.6
  1.9 0.7 copy-done.7
  2.6 13.6 %whiten.1 = (bf16[32,192,256]{2,1,0:T(8,128)(2,1)S(1)}, bf16[32,256,192]{2,1,0:T(8,128)(2,1)S(1)}) custom-call(bf16[32,2,96,256]{3,2,1,0:T(8,128)(2,1)S(1)} %copy-done.6, s32[1,256]{1,0:T(1,128)S(1)} %copy-done.7), custom_call_target="tpu_custom_call" | custom-call | tf_op jit(solution)/shard_map/whiten/pallas_call | solution.py:68
  16.1 0.0 copy-start
  16.2 2.0 copy-done
  18.2 3.5 collective-permute-start.2
  21.6 2.4 collective-permute-start.1
  24.0 65.9 %collective-permute-done.2.refs_2_ = bf16[32,192,256]{2,1,0:T(8,128)(2,1)S(1)} collective-permute-done((bf16[32,192,256]{2,1,0:T(8,128)(2,1)S(1)}, bf16[32,192,256]{2,1,0:T(8,128)(2,1)S(1)}, u32[]{:S(2)}, u32[]{:S(2)}) %collective-permute-start.2) | collective-permute-done | bytes 3145760 | tf_op jit(solution)/shard_map/ppermute | solution.py:152
  89.9 3.5 collective-permute-start.4
  93.4 5.9 %collective-permute-start.3 = (bf16[32,192,256]{2,1,0:T(8,128)(2,1)}, bf16[32,192,256]{2,1,0:T(8,128)(2,1)}, u32[]{:S(2)}, u32[]{:S(2)}) collective-permute-start(bf16[32,192,256]{2,1,0:T(8,128)(2,1)} %collective-permute-done.1.refs_1_), channel_id=1, source_target_pairs={{8,0},{12,4},{16,8},{20,12},{9,1},{13,5},{17,9},{21,13},{10,2},{14... | collective-permute-start | bytes 9437192 | tf_op jit(solution)/shard_map/ppermute | solution.py:152
  99.2 0.5 collective-permute-start
  99.8 3.4 collective-permute-start.6
  103.2 57.8 %collective-permute-done.4.refs_4_ = bf16[32,192,256]{2,1,0:T(8,128)(2,1)} collective-permute-done((bf16[32,192,256]{2,1,0:T(8,128)(2,1)S(1)}, bf16[32,192,256]{2,1,0:T(8,128)(2,1)}, u32[]{:S(2)}, u32[]{:S(2)}) %collective-permute-start.4) | collective-permute-done | bytes 3145760 | tf_op jit(solution)/shard_map/ppermute | solution.py:152
  160.9 5.0 %collective-permute-start.8 = (bf16[32,192,256]{2,1,0:T(8,128)(2,1)}, bf16[32,192,256]{2,1,0:T(8,128)(2,1)}, u32[]{:S(2)}, u32[]{:S(2)}) collective-permute-start(bf16[32,192,256]{2,1,0:T(8,128)(2,1)} %collective-permute-done.4.refs_4_), channel_id=1, source_target_pairs={{16,24},{20,28},{17,25},{21,29},{18,26},{22,30},{19,27},{23,31}} | collective-permute-start | bytes 9437192 | tf_op jit(solution)/shard_map/ppermute | solution.py:152
  166.0 0.0 collective-permute-done.3.refs_3_
  166.0 2.3 collective-permute-start.7
  168.3 2.4 collective-permute-start.5
  170.8 1.7 copy-done.1
  172.5 3.4 collective-permute-start.10
  175.9 61.8 %collective-permute-done.6.refs_6_ = bf16[32,192,256]{2,1,0:T(8,128)(2,1)S(1)} collective-permute-done((bf16[32,192,256]{2,1,0:T(8,128)(2,1)S(1)}, bf16[32,192,256]{2,1,0:T(8,128)(2,1)S(1)}, u32[]{:S(2)}, u32[]{:S(2)}) %collective-permute-start.6) | collective-permute-done | bytes 3145760 | tf_op jit(solution)/shard_map/ppermute | solution.py:152
  237.7 1.7 copy-done.8
  239.4 2.3 collective-permute-start.9
  241.8 0.1 fusion.5
  241.9 0.1 fusion.4
  241.9 3.1 multiply_convert_fusion
  245.0 8.8 %convert_element_type.96.table_ref = bf16[256,1024]{1,0:T(8,128)(2,1)} reshape(bf16[16,16,64,16]{3,2,1,0:T(8,128)(2,1)} %multiply_convert_fusion) | data formatting | bytes 1048576 | tf_op jit(solution)/shard_map/convert_element_type | solution.py:193
  253.9 0.2 select_reduce_fusion
  254.1 2.3 collective-permute-start.18
  256.4 2.3 collective-permute-start.17
  258.7 0.2 convert_reduce_fusion
  258.9 0.7 fusion.17
  259.6 0.6 add_add_fusion.3.info_ref
  260.2 0.6 add_add_fusion.2.info_ref
  260.9 0.7 add_add_fusion.1.info_ref
  261.6 0.6 add_add_fusion.info_ref
  262.2 43.0 %collective-permute-done.5.refs_5_ = bf16[32,192,256]{2,1,0:T(8,128)(2,1)} collective-permute-done((bf16[32,192,256]{2,1,0:T(8,128)(2,1)}, bf16[32,192,256]{2,1,0:T(8,128)(2,1)}, u32[]{:S(2)}, u32[]{:S(2)}) %collective-permute-start.5) | collective-permute-done | bytes 3145760 | tf_op jit(solution)/shard_map/ppermute | solution.py:152
  305.2 1.9 copy-done.2
  307.1 1.0 copy-done.4
  308.1 14.9 %correlate.6 = (f32[2,64,16,256]{3,2,1,0:T(8,128)S(1)}, bf16[2,64,16,256]{3,2,1,0:T(8,128)(2,1)S(1)}) custom-call(s32[3]{0:T(128)S(1)} %add_add_fusion.2.info_ref, bf16[32,256,192]{2,1,0:T(8,128)(2,1)} %copy-done, bf16[256,1024]{1,0:T(8,128)(2,1)S(1)} %copy-done.4, bf16[32,192,256]{2,1,0:T(8,128)(2,1)S(1)} %copy-done.2, ...), custom_call_target="tpu_custom_call" | custom-call | flops 8000000000 | bytes 12000000 | tf_op jit(solution)/shard_map/correlate/pallas_call | solution.py:125
  323.0 0.1 collective-permute-start.15
  323.1 47.0 %collective-permute-done.10.refs_10_ = bf16[32,192,256]{2,1,0:T(8,128)(2,1)} collective-permute-done((bf16[32,192,256]{2,1,0:T(8,128)(2,1)}, bf16[32,192,256]{2,1,0:T(8,128)(2,1)}, u32[]{:S(2)}, u32[]{:S(2)}) %collective-permute-start.10) | collective-permute-done | bytes 3145760 | tf_op jit(solution)/shard_map/ppermute | solution.py:152
  370.1 15.8 %correlate.4 = (f32[2,64,16,256]{3,2,1,0:T(8,128)S(1)}, bf16[2,64,16,256]{3,2,1,0:T(8,128)(2,1)}) custom-call(s32[3]{0:T(128)S(1)} %add_add_fusion.info_ref, bf16[32,256,192]{2,1,0:T(8,128)(2,1)} %copy-done, bf16[256,1024]{1,0:T(8,128)(2,1)S(1)} %copy-done.4, bf16[32,192,256]{2,1,0:T(8,128)(2,1)S(1)} %copy-done.2, ...), custom_call_target="tpu_custom_call" | custom-call | flops 8000000000 | bytes 12000000 | tf_op jit(solution)/shard_map/correlate/pallas_call | solution.py:125
  386.0 0.1 collective-permute-start.11
  386.0 14.3 %correlate.5 = (f32[2,64,16,256]{3,2,1,0:T(8,128)S(1)}, bf16[2,64,16,256]{3,2,1,0:T(8,128)(2,1)}) custom-call(s32[3]{0:T(128)S(1)} %add_add_fusion.1.info_ref, bf16[32,256,192]{2,1,0:T(8,128)(2,1)} %copy-done, bf16[256,1024]{1,0:T(8,128)(2,1)S(1)} %copy-done.4, bf16[32,192,256]{2,1,0:T(8,128)(2,1)S(1)} %copy-done.2, ...), custom_call_target="tpu_custom_call" | custom-call | flops 8000000000 | bytes 12000000 | tf_op jit(solution)/shard_map/correlate/pallas_call | solution.py:125
  400.4 0.4 collective-permute-start.13
  400.8 14.9 %correlate.7 = (f32[2,64,16,256]{3,2,1,0:T(8,128)S(1)}, bf16[2,64,16,256]{3,2,1,0:T(8,128)(2,1)S(1)}) custom-call(s32[3]{0:T(128)S(1)} %add_add_fusion.3.info_ref, bf16[32,256,192]{2,1,0:T(8,128)(2,1)} %copy-done, bf16[256,1024]{1,0:T(8,128)(2,1)S(1)} %copy-done.5, bf16[32,192,256]{2,1,0:T(8,128)(2,1)S(1)} %copy-done.3, ...), custom_call_target="tpu_custom_call" | custom-call | flops 8000000000 | bytes 12000000 | tf_op jit(solution)/shard_map/correlate/pallas_call | solution.py:125
  415.7 0.2 collective-permute-start.19
  416.0 0.2 fusion.2
  416.2 0.6 collective-permute-start.16
  416.7 0.2 fusion
  416.9 1.6 collective-permute-start.12
  418.5 0.2 fusion.1
  418.8 0.6 collective-permute-start.14
  419.3 0.2 fusion.3
  419.5 1.6 collective-permute-start.20
  421.1 0.7 fusion.18
  429.7 1.3 collective-permute-done.16
  431.0 11.2 %collective-permute-done.12 = bf16[64,16,256]{2,1,0:T(8,128)(2,1)S(1)} collective-permute-done((bf16[64,16,256]{2,1,0:T(8,128)(2,1)S(1)}, bf16[64,16,256]{2,1,0:T(8,128)(2,1)S(1)}, u32[]{:S(2)}, u32[]{:S(2)}) %collective-permute-start.12) | collective-permute-done | bytes 524320 | tf_op jit(solution)/shard_map/ppermute | solution.py:225
  442.2 11.2 %collective-permute-done.14 = bf16[64,16,256]{2,1,0:T(8,128)(2,1)S(1)} collective-permute-done((bf16[64,16,256]{2,1,0:T(8,128)(2,1)S(1)}, bf16[64,16,256]{2,1,0:T(8,128)(2,1)S(1)}, u32[]{:S(2)}, u32[]{:S(2)}) %collective-permute-start.14) | collective-permute-done | bytes 524320 | tf_op jit(solution)/shard_map/ppermute | solution.py:225
  453.4 10.7 %collective-permute-done.20 = bf16[64,16,256]{2,1,0:T(8,128)(2,1)S(1)} collective-permute-done((bf16[64,16,256]{2,1,0:T(8,128)(2,1)S(1)}, bf16[64,16,256]{2,1,0:T(8,128)(2,1)S(1)}, u32[]{:S(2)}, u32[]{:S(2)}) %collective-permute-start.20) | collective-permute-done | bytes 524320 | tf_op jit(solution)/shard_map/ppermute | solution.py:225
  464.1 1.1 select_bitcast_fusion.3
  465.2 0.5 select_bitcast_fusion.2
  465.7 0.5 maximum_bitcast_fusion
  466.3 2.7 copy.6
  (27 shorter events, 0.1 us)
Async XLA Ops:
  0.0 1.9 copy-start.6
  1.9 0.7 copy-start.7
  16.1 2.0 copy-start
  18.2 71.7 %collective-permute-start.2 = (bf16[32,192,256]{2,1,0:T(8,128)(2,1)S(1)}, bf16[32,192,256]{2,1,0:T(8,128)(2,1)S(1)}, u32[]{:S(2)}, u32[]{:S(2)}) collective-permute-start(bf16[32,192,256]{2,1,0:T(8,128)(2,1)S(1)} %get-tuple-element.16), channel_id=1, source_target_pairs={{0,8},{4,12},{8,16},{12,20},{16,24},{20,28},{1,9},{5,13},{9,17},{1... | collective-permute-start | bytes 9437192 | tf_op jit(solution)/shard_map/ppermute | solution.py:152
  21.6 71.7 %collective-permute-start.1 = (bf16[32,192,256]{2,1,0:T(8,128)(2,1)S(1)}, bf16[32,192,256]{2,1,0:T(8,128)(2,1)}, u32[]{:S(2)}, u32[]{:S(2)}) collective-permute-start(bf16[32,192,256]{2,1,0:T(8,128)(2,1)S(1)} %get-tuple-element.16), channel_id=1, source_target_pairs={{8,0},{12,4},{16,8},{20,12},{24,16},{28,20},{9,1},{13,5},{17,9},{2... | collective-permute-start | bytes 9437192 | tf_op jit(solution)/shard_map/ppermute | solution.py:152
  89.9 71.1 %collective-permute-start.4 = (bf16[32,192,256]{2,1,0:T(8,128)(2,1)S(1)}, bf16[32,192,256]{2,1,0:T(8,128)(2,1)}, u32[]{:S(2)}, u32[]{:S(2)}) collective-permute-start(bf16[32,192,256]{2,1,0:T(8,128)(2,1)S(1)} %collective-permute-done.2.refs_2_), channel_id=1, source_target_pairs={{8,16},{12,20},{16,24},{20,28},{9,17},{13,21},{17,25},{21,29},{10,... | collective-permute-start | bytes 9437192 | tf_op jit(solution)/shard_map/ppermute | solution.py:152
  93.4 72.6 %collective-permute-start.3 = (bf16[32,192,256]{2,1,0:T(8,128)(2,1)}, bf16[32,192,256]{2,1,0:T(8,128)(2,1)}, u32[]{:S(2)}, u32[]{:S(2)}) collective-permute-start(bf16[32,192,256]{2,1,0:T(8,128)(2,1)} %collective-permute-done.1.refs_1_), channel_id=1, source_target_pairs={{8,0},{12,4},{16,8},{20,12},{9,1},{13,5},{17,9},{21,13},{10,2},{14... | collective-permute-start | bytes 9437192 | tf_op jit(solution)/shard_map/ppermute | solution.py:152
  99.2 71.5 %collective-permute-start = (bf16[32,192,256]{2,1,0:T(8,128)(2,1)S(1)}, bf16[32,192,256]{2,1,0:T(8,128)(2,1)S(1)}, u32[]{:S(2)}, u32[]{:S(2)}) collective-permute-start(bf16[32,192,256]{2,1,0:T(8,128)(2,1)S(1)} %get-tuple-element.16), channel_id=1, source_target_pairs={{0,4},{4,0},{8,12},{12,8},{16,20},{20,16},{24,28},{28,24},{1,5},{5... | collective-permute-start | bytes 9437192 | tf_op jit(solution)/shard_map/ppermute | solution.py:152
  99.8 137.9 %collective-permute-start.6 = (bf16[32,192,256]{2,1,0:T(8,128)(2,1)S(1)}, bf16[32,192,256]{2,1,0:T(8,128)(2,1)S(1)}, u32[]{:S(2)}, u32[]{:S(2)}) collective-permute-start(bf16[32,192,256]{2,1,0:T(8,128)(2,1)S(1)} %collective-permute-done.2.refs_2_), channel_id=1, source_target_pairs={{8,12},{12,8},{16,20},{20,16},{24,28},{28,24},{9,13},{13,9},{17,21... | collective-permute-start | bytes 9437192 | tf_op jit(solution)/shard_map/ppermute | solution.py:152
  160.9 93.1 %collective-permute-start.8 = (bf16[32,192,256]{2,1,0:T(8,128)(2,1)}, bf16[32,192,256]{2,1,0:T(8,128)(2,1)}, u32[]{:S(2)}, u32[]{:S(2)}) collective-permute-start(bf16[32,192,256]{2,1,0:T(8,128)(2,1)} %collective-permute-done.4.refs_4_), channel_id=1, source_target_pairs={{16,24},{20,28},{17,25},{21,29},{18,26},{22,30},{19,27},{23,31}} | collective-permute-start | bytes 9437192 | tf_op jit(solution)/shard_map/ppermute | solution.py:152
  166.0 90.4 %collective-permute-start.7 = (bf16[32,192,256]{2,1,0:T(8,128)(2,1)}, bf16[32,192,256]{2,1,0:T(8,128)(2,1)}, u32[]{:S(2)}, u32[]{:S(2)}) collective-permute-start(bf16[32,192,256]{2,1,0:T(8,128)(2,1)} %collective-permute-done.3.refs_3_), channel_id=1, source_target_pairs={{8,0},{12,4},{9,1},{13,5},{10,2},{14,6},{11,3},{15,7}} | collective-permute-start | bytes 9437192 | tf_op jit(solution)/shard_map/ppermute | solution.py:152
  168.3 136.9 %collective-permute-start.5 = (bf16[32,192,256]{2,1,0:T(8,128)(2,1)}, bf16[32,192,256]{2,1,0:T(8,128)(2,1)}, u32[]{:S(2)}, u32[]{:S(2)}) collective-permute-start(bf16[32,192,256]{2,1,0:T(8,128)(2,1)} %collective-permute-done.1.refs_1_), channel_id=1, source_target_pairs={{0,4},{4,0},{8,12},{12,8},{16,20},{20,16},{1,5},{5,1},{9,13},{13,9... | collective-permute-start | bytes 9437192 | tf_op jit(solution)/shard_map/ppermute | solution.py:152
  170.8 1.7 copy-start.1
  172.5 197.6 %collective-permute-start.10 = (bf16[32,192,256]{2,1,0:T(8,128)(2,1)}, bf16[32,192,256]{2,1,0:T(8,128)(2,1)}, u32[]{:S(2)}, u32[]{:S(2)}) collective-permute-start(bf16[32,192,256]{2,1,0:T(8,128)(2,1)} %collective-permute-done.4.refs_4_), channel_id=1, source_target_pairs={{16,20},{20,16},{24,28},{28,24},{17,21},{21,17},{25,29},{29,25},{1... | collective-permute-start | bytes 9437192 | tf_op jit(solution)/shard_map/ppermute | solution.py:152
  237.7 1.7 copy-start.8
  239.4 130.7 %collective-permute-start.9 = (bf16[32,192,256]{2,1,0:T(8,128)(2,1)}, bf16[32,192,256]{2,1,0:T(8,128)(2,1)}, u32[]{:S(2)}, u32[]{:S(2)}) collective-permute-start(bf16[32,192,256]{2,1,0:T(8,128)(2,1)} %collective-permute-done.3.refs_3_), channel_id=1, source_target_pairs={{0,4},{4,0},{8,12},{12,8},{1,5},{5,1},{9,13},{13,9},{2,6},{6,2},{1... | collective-permute-start | bytes 9437192 | tf_op jit(solution)/shard_map/ppermute | solution.py:152
  245.0 8.8 %copy-start.9 = (s32[4,8]{1,0:T(4,128)S(1)}, s32[4,8]{1,0:T(4,128)}, u32[]{:S(2)}) copy-start(s32[4,8]{1,0:T(4,128)} %param.5) | copy-start | bytes 388
  254.1 146.7 %collective-permute-start.18 = (bf16[32,192,256]{2,1,0:T(8,128)(2,1)}, bf16[32,192,256]{2,1,0:T(8,128)(2,1)}, u32[]{:S(2)}, u32[]{:S(2)}) collective-permute-start(bf16[32,192,256]{2,1,0:T(8,128)(2,1)} %collective-permute-done.8.refs_8_), channel_id=1, source_target_pairs={{24,28},{28,24},{25,29},{29,25},{26,30},{30,26},{27,31},{31,27}} | collective-permute-start | bytes 9437192 | tf_op jit(solution)/shard_map/ppermute | solution.py:152
  256.4 144.4 %collective-permute-start.17 = (bf16[32,192,256]{2,1,0:T(8,128)(2,1)}, bf16[32,192,256]{2,1,0:T(8,128)(2,1)}, u32[]{:S(2)}, u32[]{:S(2)}) collective-permute-start(bf16[32,192,256]{2,1,0:T(8,128)(2,1)} %collective-permute-done.7.refs_7_), channel_id=1, source_target_pairs={{0,4},{4,0},{1,5},{5,1},{2,6},{6,2},{3,7},{7,3}} | collective-permute-start | bytes 9437192 | tf_op jit(solution)/shard_map/ppermute | solution.py:152
  305.2 1.9 copy-start.2
  307.1 1.0 copy-start.4
  323.0 92.9 %collective-permute-start.15 = (bf16[2,64,16,256]{3,2,1,0:T(8,128)(2,1)S(1)}, bf16[2,64,16,256]{3,2,1,0:T(8,128)(2,1)S(1)}, u32[]{:S(2)}, u32[]{:S(2)}) collective-permute-start(bf16[2,64,16,256]{3,2,1,0:T(8,128)(2,1)S(1)} %get-tuple-element.22), channel_id=1, source_target_pairs={{0,1},{1,0},{2,3},{3,2},{4,5},{5,4},{6,7},{7,6},{8,9},{9,8},{10,11... | collective-permute-start | bytes 3145736 | tf_op jit(solution)/shard_map/ppermute | solution.py:223
  385.9 14.9 %copy-start.3 = (bf16[32,192,256]{2,1,0:T(8,128)(2,1)S(1)}, bf16[32,192,256]{2,1,0:T(8,128)(2,1)}, u32[]{:S(2)}) copy-start(bf16[32,192,256]{2,1,0:T(8,128)(2,1)} %copy-done.1) | copy-start | bytes 9437188
  386.0 14.8 %copy-start.5 = (bf16[256,1024]{1,0:T(8,128)(2,1)S(1)}, bf16[256,1024]{1,0:T(8,128)(2,1)}, u32[]{:S(2)}) copy-start(bf16[256,1024]{1,0:T(8,128)(2,1)} %convert_element_type.96.table_ref) | copy-start | bytes 1572868
  386.0 30.8 %collective-permute-start.11 = (bf16[2,64,16,256]{3,2,1,0:T(8,128)(2,1)}, bf16[2,64,16,256]{3,2,1,0:T(8,128)(2,1)S(1)}, u32[]{:S(2)}, u32[]{:S(2)}) collective-permute-start(bf16[2,64,16,256]{3,2,1,0:T(8,128)(2,1)} %get-tuple-element.18), channel_id=1, source_target_pairs={{0,1},{1,0},{2,3},{3,2},{4,5},{5,4},{6,7},{7,6},{8,9},{9,8},{10,11... | collective-permute-start | bytes 3145736 | tf_op jit(solution)/shard_map/ppermute | solution.py:223
  400.4 18.2 %collective-permute-start.13 = (bf16[2,64,16,256]{3,2,1,0:T(8,128)(2,1)}, bf16[2,64,16,256]{3,2,1,0:T(8,128)(2,1)S(1)}, u32[]{:S(2)}, u32[]{:S(2)}) collective-permute-start(bf16[2,64,16,256]{3,2,1,0:T(8,128)(2,1)} %get-tuple-element.20), channel_id=1, source_target_pairs={{0,1},{1,0},{2,3},{3,2},{4,5},{5,4},{6,7},{7,6},{8,9},{9,8},{10,11... | collective-permute-start | bytes 3145736 | tf_op jit(solution)/shard_map/ppermute | solution.py:223
  415.7 3.6 collective-permute-start.19
  416.2 14.8 %collective-permute-start.16 = (bf16[64,16,256]{2,1,0:T(8,128)(2,1)S(1)}, bf16[64,16,256]{2,1,0:T(8,128)(2,1)S(1)}, u32[]{:S(2)}, u32[]{:S(2)}) collective-permute-start(bf16[64,16,256]{2,1,0:T(8,128)(2,1)S(1)} %fusion.2), channel_id=1, source_target_pairs={{0,2},{1,3},{2,0},{3,1},{4,6},{5,7},{6,4},{7,5},{8,10},{9,11},{10,... | collective-permute-start | bytes 1572872 | tf_op jit(solution)/shard_map/ppermute | solution.py:225
  416.9 25.3 %collective-permute-start.12 = (bf16[64,16,256]{2,1,0:T(8,128)(2,1)S(1)}, bf16[64,16,256]{2,1,0:T(8,128)(2,1)S(1)}, u32[]{:S(2)}, u32[]{:S(2)}) collective-permute-start(bf16[64,16,256]{2,1,0:T(8,128)(2,1)S(1)} %fusion), channel_id=1, source_target_pairs={{0,2},{1,3},{2,0},{3,1},{4,6},{5,7},{6,4},{7,5},{8,10},{9,11},{10,... | collective-permute-start | bytes 1572872 | tf_op jit(solution)/shard_map/ppermute | solution.py:225
  418.8 34.7 %collective-permute-start.14 = (bf16[64,16,256]{2,1,0:T(8,128)(2,1)S(1)}, bf16[64,16,256]{2,1,0:T(8,128)(2,1)S(1)}, u32[]{:S(2)}, u32[]{:S(2)}) collective-permute-start(bf16[64,16,256]{2,1,0:T(8,128)(2,1)S(1)} %fusion.1), channel_id=1, source_target_pairs={{0,2},{1,3},{2,0},{3,1},{4,6},{5,7},{6,4},{7,5},{8,10},{9,11},{10,... | collective-permute-start | bytes 1572872 | tf_op jit(solution)/shard_map/ppermute | solution.py:225
  419.5 44.6 %collective-permute-start.20 = (bf16[64,16,256]{2,1,0:T(8,128)(2,1)S(1)}, bf16[64,16,256]{2,1,0:T(8,128)(2,1)S(1)}, u32[]{:S(2)}, u32[]{:S(2)}) collective-permute-start(bf16[64,16,256]{2,1,0:T(8,128)(2,1)S(1)} %fusion.3), channel_id=1, source_target_pairs={{0,2},{1,3},{2,0},{3,1},{4,6},{5,7},{6,4},{7,5},{8,10},{9,11},{10,... | collective-permute-start | bytes 1572872 | tf_op jit(solution)/shard_map/ppermute | solution.py:225

commit v2 on v1

--- a/solution.py
+++ b/solution.py
@@ -1,4 +1,3 @@
-import functools
 import math
 
 import jax
@@ -144,43 +143,312 @@
     )(info, lhs, table, *mates)
 
 
-def gather_blocks(own, blocks):
-    chain = blocks // 2
-    got = {}
-
-    def send(block, pairs):
-        return lax.ppermute(block, "pair", pairs)
-
-    def chain_pairs(step, depth):
-        links = []
-        for c in range(chain):
-            src = c + step
-            if 0 <= c + step * depth < chain:
-                links += [(2 * src + x, 2 * c + x) for x in range(2)]
-        return links
-
-    def swap_pairs(reach):
-        return [
-            (2 * c + x, 2 * c + 1 - x)
-            for c in range(chain)
-            if 0 <= c + reach < chain
-            for x in range(2)
-        ]
-
-    got[(0, 1)] = send(own, swap_pairs(0))
-    for depth in range(1, chain):
-        for step in (1, -1):
-            before = own if depth == 1 else got[(step * (depth - 1), 0)]
-            got[(step * depth, 0)] = send(before, chain_pairs(step, depth))
-    for depth in range(1, chain):
-        for step in (1, -1):
-            got[(step * depth, 1)] = send(got[(step * depth, 0)], swap_pairs(step * depth))
-    return got
-
-
-ARRIVAL = [(0, 1), (1, 0), (-1, 0), (2, 0), (-2, 0), (1, 1), (-1, 1)]
-ARRIVAL += [(3, 0), (-3, 0), (2, 1), (-2, 1), (3, 1), (-3, 1)]
-READY = (7, 9, 11, 13)
+CHAIN = 4
+HALVES = 2
+ARRIVAL = (
+    ((0, 1), (1, 0), (1, 1), (2, 0), (3, 0), (2, 1), (3, 1)),
+    ((1, 1), (0, 0), (2, 0), (0, 1), (3, 0), (2, 1), (3, 1)),
+    ((2, 1), (3, 0), (1, 0), (3, 1), (0, 0), (1, 1), (0, 1)),
+    ((3, 1), (2, 0), (2, 1), (1, 0), (0, 0), (1, 1), (0, 1)),
+)
+STEPS = 8
+TURN_AFTER = {4: (0,), 6: (1, 2), 7: (3,)}
+
+
+def plan_links():
+    last = CHAIN - 1
+    queue = {}
+    for c in range(CHAIN):
+        down = [(b, 0, h) for b in range(c, CHAIN) for h in range(HALVES)] + [(last, 1, 1)]
+        up = [(b, 0, h) for b in range(c, -1, -1) for h in range(HALVES)] + [(0, 1, 1)]
+        if c > 0:
+            queue[c, "down"] = down
+        if c < last:
+            queue[c, "up"] = up
+        near = [b for b in (range(c + 1, CHAIN) if c == 0 else range(c - 1, -1, -1))]
+        if c == 1:
+            near = [0, 2, 3]
+        if c == 2:
+            near = [3, 1, 0]
+        swap = [(c, 0, 0), (c, 0, 1)]
+        for b in near:
+            by_chain = (b == last and c < last) or (b == 0 and c > 0)
+            swap += [(b, 0, h) for h in range(HALVES) if not (by_chain and h == 1)]
+        queue[c, "swap"] = swap
+    have = {(c, (c, 0, h)): 0 for c in range(CHAIN) for h in range(HALVES)}
+    start = {key: [] for key in queue}
+    for t in range(STEPS):
+        new = {}
+        for (c, way), items in queue.items():
+            at = len(start[c, way])
+            if at < len(items) and have.get((c, items[at]), 99) <= t:
+                start[c, way].append(t)
+                b, sw, h = items[at]
+                if way == "swap":
+                    new[c, (b, 1 - sw, h)] = t + 1
+                else:
+                    new[c + (1 if way == "up" else -1), (b, sw, h)] = t + 1
+        for key, when in new.items():
+            assert key not in have
+            have[key] = when
+    waits = {(c, t): [] for c in range(CHAIN) for t in range(STEPS)}
+    sends = {(c, t): [] for c in range(CHAIN) for t in range(STEPS)}
+    for (c, item), when in have.items():
+        if when > 0:
+            waits[c, when].append(item)
+    for (c, way), items in queue.items():
+        assert len(start[c, way]) == len(items)
+        for item, t in zip(items, start[c, way]):
+            sends[c, max(t - 1, have[c, item], 0)].append((way, item))
+    for c in range(CHAIN):
+        for k in range(ROUNDS):
+            step = [t for t, turns in TURN_AFTER.items() if k in turns][0]
+            for b, sw in ARRIVAL[c][k : k + 4]:
+                for h in range(HALVES):
+                    assert have[c, (b, sw, h)] <= step
+    return waits, sends
+
+
+def fused_kernel(
+    pick_ref, spec_ref, order_ref, table_ref, out_ref,
+    blocks, lhs, cross, keep, give, beside, passed, across,
+    swap_sem, chain_sem, got_sem, give_sem, beside_sem, passed_sem, across_sem,
+):
+    nf, _, nw, nc = spec_ref.shape
+    part = nf // HALVES
+    share = nc // 4
+    lag_rows = share * LAGS
+    pair = lax.axis_index("pair")
+    win = lax.axis_index("win")
+    c, x = pair // 2, pair % 2
+    row, core = win // 2, win % 2
+    swap_to = {"pair": pair + 1 - 2 * x}
+    core_to = {"win": win + 1 - 2 * core}
+    row_to = {"win": win + 2 - 4 * row}
+    waits, sends = plan_links()
+
+    def signal(to):
+        pl.semaphore_signal(
+            pltpu.get_barrier_semaphore(), inc=1, device_id=to,
+            device_id_type=pl.DeviceIdType.MESH,
+        )
+
+    signal(swap_to)
+    signal(core_to)
+    signal(row_to)
+
+    @pl.when(c > 0)
+    def _():
+        signal({"pair": pair - 2})
+
+    @pl.when(c < CHAIN - 1)
+    def _():
+        signal({"pair": pair + 2})
+
+    @pl.when((c > 0) & (c < CHAIN - 1))
+    def _():
+        pl.semaphore_wait(pltpu.get_barrier_semaphore(), 5)
+
+    @pl.when((c == 0) | (c == CHAIN - 1))
+    def _():
+        pl.semaphore_wait(pltpu.get_barrier_semaphore(), 4)
+
+    def copy(way, item):
+        b, sw, h = item
+        q = 2 * b + (x if sw == 0 else 1 - x)
+        ref = blocks.at[q, pl.ds(h * part, part)]
+        if way == "swap":
+            sem, to = swap_sem.at[b, h], swap_to
+        else:
+            side = 0 if way == "down" else 1
+            sem = chain_sem.at[side, 2 * b + sw, h]
+            to = {"pair": pair - 2 if way == "down" else pair + 2}
+        return pltpu.make_async_remote_copy(
+            src_ref=ref, dst_ref=ref, send_sem=sem, recv_sem=got_sem.at[q, h],
+            device_id=to, device_id_type=pl.DeviceIdType.MESH,
+        )
+
+    def links(t, only=None):
+        for cs in range(CHAIN):
+
+            @pl.when(c == cs)
+            def _(cs=cs):
+                if only in (None, 0):
+                    for item in waits[cs, t]:
+                        copy("swap", item).wait_recv()
+                for way, item in sends[cs, t]:
+                    if only is None or item[2] == only:
+                        copy(way, item).start()
+
+    def square(f, carry):
+        re = spec_ref[f, 0].astype(F32)
+        im = spec_ref[f, 1].astype(F32)
+        out_ref[pl.ds(pl.multiple_of((f + 2) * nw, 8), nw)] = re * re + im * im
+        return carry
+
+    zero = jnp.zeros((nw, nc), F32)
+    for edge in (0, 1, nf + 2, nf + 3):
+        out_ref[pl.ds(edge * nw, nw)] = zero
+    lax.fori_loop(0, nf, square, 0)
+    rows = lax.broadcasted_iota(jnp.int32, (nc, nc), 0)
+    cols = lax.broadcasted_iota(jnp.int32, (nc, nc), 1)
+
+    def scale(f, carry):
+        pick = (rows == order_ref[...]).astype(F32).astype(BF)
+        total = out_ref[pl.ds(pl.multiple_of(f * nw, 8), nw)]
+        for d in range(1, 5):
+            total += out_ref[pl.ds(pl.multiple_of((f + d) * nw, 8), nw)]
+        count = jnp.minimum(f + 2, nf - 1) - jnp.maximum(f - 2, 0) + 1
+        mean = total / count.astype(F32)
+        inv = 1.0 / jnp.maximum(jnp.sqrt(mean), 0.5)
+        white = jnp.concatenate(
+            [
+                (spec_ref[f, 0].astype(F32) * inv).astype(BF),
+                (spec_ref[f, 1].astype(F32) * inv).astype(BF),
+            ],
+            0,
+        )
+        blocks[pair, f] = jnp.dot(white, pick, preferred_element_type=F32).astype(BF)
+        return carry
+
+    for h in range(HALVES):
+        lax.fori_loop(h * part, (h + 1) * part, scale, 0)
+        links(0, h)
+
+    def turn_bin(f, carry):
+        eye = (rows == cols).astype(F32).astype(BF)
+        turned = lax.dot_general(
+            eye, blocks[pair, f], (((1,), (1,)), ((), ())), preferred_element_type=F32
+        )
+        lhs[f] = turned.astype(BF)
+        return carry
+
+    lax.fori_loop(0, nf, turn_bin, 0)
+
+    def to_core(k):
+        return pltpu.make_async_remote_copy(
+            src_ref=give.at[k % 2], dst_ref=beside.at[k], send_sem=give_sem.at[k],
+            recv_sem=beside_sem.at[k], device_id=core_to,
+            device_id_type=pl.DeviceIdType.MESH,
+        )
+
+    def to_row(k):
+        return pltpu.make_async_remote_copy(
+            src_ref=passed.at[k], dst_ref=across.at[k], send_sem=passed_sem.at[k],
+            recv_sem=across_sem.at[k], device_id=row_to,
+            device_id_type=pl.DeviceIdType.MESH,
+        )
+
+    def correlate_turn(k):
+        places = []
+        for m in range(4):
+            at = jnp.int32(0)
+            for cs in range(CHAIN):
+                b, sw = ARRIVAL[cs][k + m]
+                at = at + (c == cs).astype(jnp.int32) * (2 * b + (x if sw == 0 else 1 - x))
+            places.append(at)
+
+        def one_bin(f, carry):
+            right = None
+            for m in range(4):
+                weight = (pick_ref[k] == m).astype(F32)
+                term = blocks[places[m], f] * jnp.full((1, nc), weight, F32).astype(BF)
+                right = term if right is None else right + term
+            turned = jnp.concatenate([right[nw:], -right[:nw]], 0)
+            left = lhs[f]
+            cross[f] = jnp.dot(left, right, preferred_element_type=F32).astype(BF)
+            cross[nf + f] = jnp.dot(left, turned, preferred_element_type=F32).astype(BF)
+            return carry
+
+        lax.fori_loop(0, nf, one_bin, 0)
+        if k >= 2:
+            to_core(k - 2).wait_send()
+
+        def lags_of(half, other, u):
+            owner = lax.rem(row + half, 2) * 2 + lax.rem(core + other, 2)
+            start = pl.multiple_of(owner * share + u * GROUP, GROUP)
+            right = cross[:, pl.ds(start, GROUP), :].reshape(2 * nf * GROUP, nc)
+            return jnp.dot(table_ref[...], right, preferred_element_type=F32)
+
+        size = GROUP * LAGS
+
+        def send_group(u, carry):
+            for half in range(2):
+                at = pl.multiple_of(half * lag_rows + u * size, size)
+                give[k % 2, pl.ds(at, size)] = lags_of(half, 1, u).astype(BF)
+            return carry
+
+        def keep_group(u, carry):
+            at = pl.multiple_of(u * size, size)
+            keep[pl.ds(at, size)] = lags_of(1, 0, u)
+            to = pl.multiple_of(k * lag_rows + u * size, size)
+            out_ref[pl.ds(to, size)] = lags_of(0, 0, u)
+            return carry
+
+        lax.fori_loop(0, share // GROUP, send_group, 0)
+        to_core(k).start()
+        lax.fori_loop(0, share // GROUP, keep_group, 0)
+        to_core(k).wait_recv()
+        passed[k] = (keep[...] + beside[k, pl.ds(lag_rows, lag_rows)].astype(F32)).astype(BF)
+        to_row(k).start()
+        out_ref[pl.ds(k * lag_rows, lag_rows)] += beside[k, pl.ds(0, lag_rows)].astype(F32)
+
+    for t in range(1, STEPS):
+        links(t)
+        for k in TURN_AFTER.get(t, ()):
+            correlate_turn(k)
+    for k in range(ROUNDS):
+        to_row(k).wait_recv()
+        out_ref[pl.ds(k * lag_rows, lag_rows)] += across[k].astype(F32)
+    for k in range(ROUNDS):
+        if k >= 2:
+            to_core(k).wait_send()
+        to_row(k).wait_send()
+    for cs in range(CHAIN):
+
+        @pl.when(c == cs)
+        def _(cs=cs):
+            for t in range(STEPS):
+                for way, item in sends[cs, t]:
+                    copy(way, item).wait_send()
+
+
+def fused(pick, spectra, order, table):
+    nf, _, nw, nc = spectra.shape
+    blocks = lax.axis_size("pair")
+    rows = nc // 4 * LAGS
+    vmem = pl.BlockSpec(memory_space=pltpu.VMEM)
+    dma = pltpu.SemaphoreType.DMA
+    return pl.pallas_call(
+        fused_kernel,
+        out_shape=jax.ShapeDtypeStruct((ROUNDS * rows, nc), F32),
+        in_specs=[pl.BlockSpec(memory_space=pltpu.SMEM), vmem, vmem, vmem],
+        out_specs=vmem,
+        scratch_shapes=[
+            pltpu.VMEM((blocks, nf, 2 * nw, nc), BF),
+            pltpu.VMEM((nf, nc, 2 * nw), BF),
+            pltpu.VMEM((2 * nf, nc, nc), BF),
+            pltpu.VMEM((rows, nc), F32),
+            pltpu.VMEM((2, 2 * rows, nc), BF),
+            pltpu.VMEM((ROUNDS, 2 * rows, nc), BF),
+            pltpu.VMEM((ROUNDS, rows, nc), BF),
+            pltpu.VMEM((ROUNDS, rows, nc), BF),
+            dma((CHAIN, HALVES)),
+            dma((2, 2 * CHAIN, HALVES)),
+            dma((blocks, HALVES)),
+            dma((ROUNDS,)),
+            dma((ROUNDS,)),
+            dma((ROUNDS,)),
+            dma((ROUNDS,)),
+        ],
+        cost_estimate=pl.CostEstimate(
+            flops=16_000_000_000, bytes_accessed=16_000_000, transcendentals=0
+        ),
+        compiler_params=pltpu.CompilerParams(
+            vmem_limit_bytes=60 * 2**20, collective_id=0, has_side_effects=True
+        ),
+        name="fused",
+    )(pick, spectra, order, table)
 
 
 def local(spectra, channel_order, partners):
@@ -191,49 +459,43 @@
     spread = (
         table.T[None, :, :, None] * jnp.eye(GROUP, dtype=F32)[:, None, None, :]
     ).reshape(GROUP * LAGS, 2 * nf * GROUP).astype(BF)
-    own, lhs = whiten(spectra, channel_order)
     me = lax.axis_index("pair")
     win = lax.axis_index("win")
+    if num_blocks == 2 * CHAIN and win_count == 4:
+        mine = partners[:, me]
+        rank = jnp.zeros_like(mine)
+        for c in range(CHAIN):
+            for index, (b, sw) in enumerate(ARRIVAL[c]):
+                same = (mine // 2 == b) & ((mine % 2 != me % 2) == (sw == 1))
+                rank = jnp.where((me // 2 == c) & same, index, rank)
+        place = jnp.sum((rank[None, :] < rank[:, None]).astype(jnp.int32), 1)
+        turns = jnp.arange(ROUNDS, dtype=jnp.int32)
+        pick = jnp.sum(jnp.where(place[None, :] == turns[:, None], rank[None, :], 0), 1) - turns
+        sums = fused(pick.astype(jnp.int32), spectra, channel_order, spread)
+        sums = sums.reshape(ROUNDS, nc // 4, LAGS, nc)
+        ordered = []
+        for turn in range(ROUNDS):
+            value = sums[ROUNDS - 1]
+            for k in range(ROUNDS - 1):
+                value = jnp.where(place[turn] == k, sums[k], value)
+            ordered.append(value)
+        return jnp.stack(ordered, 1)[None]
+    own, lhs = whiten(spectra, channel_order)
     row, core = win // 2, win % 2
-    mine = partners[:, me]
     results = []
-    if num_blocks == 8:
-        got = gather_blocks(own, num_blocks)
-        reach = mine // 2 - me // 2
-        column = jnp.abs(mine % 2 - me % 2)
-        rank = jnp.zeros_like(mine)
-        for index, (step, other) in enumerate(ARRIVAL):
-            rank = jnp.where((reach == step) & (column == other), index, rank)
-        place = jnp.sum((rank[None, :] < rank[:, None]).astype(jnp.int32), 1)
-    else:
-        place = None
-        turned = lax.all_to_all(
-            own.reshape(num_blocks, -1), "pair", split_axis=0, concat_axis=0, tiled=True
-        )
+    turned = lax.all_to_all(
+        own.reshape(num_blocks, -1), "pair", split_axis=0, concat_axis=0, tiled=True
+    )
     for turn in range(ROUNDS):
-        if place is None:
-            arranged = jnp.take(turned, partners[turn], axis=0)
-            received = lax.all_to_all(arranged, "pair", split_axis=0, concat_axis=0, tiled=True)
-            mates, slot = [received.reshape(own.shape)], jnp.int32(0)
-        else:
-            mates = [got[key] for key in ARRIVAL[: READY[turn]]]
-            slot = jnp.sum(jnp.where(place == turn, rank, 0))
-        info = jnp.stack([slot, core, row]).astype(jnp.int32)
-        keep, give = correlate(info, lhs, spread, mates)
+        arranged = jnp.take(turned, partners[turn], axis=0)
+        received = lax.all_to_all(arranged, "pair", split_axis=0, concat_axis=0, tiled=True)
+        info = jnp.stack([jnp.int32(0), core, row]).astype(jnp.int32)
+        keep, give = correlate(info, lhs, spread, [received.reshape(own.shape)])
         beside = lax.ppermute(give, "win", [(w, w ^ 1) for w in range(win_count)])
         passed = (keep[1] + beside[1].astype(F32)).astype(BF)
         across = lax.ppermute(passed, "win", [(w, w ^ 2) for w in range(win_count)])
         results.append(keep[0] + beside[0].astype(F32) + across.astype(F32))
-    if place is None:
-        return jnp.stack(results, 1)[None]
-    ordered = []
-    for turn in range(ROUNDS):
-        at = place[turn]
-        value = results[ROUNDS - 1]
-        for k in range(ROUNDS - 1):
-            value = jnp.where(at == k, results[k], value)
-        ordered.append(value)
-    return jnp.stack(ordered, 1)[None]
+    return jnp.stack(results, 1)[None]
 
 
 def solution(mesh):

time: 470 us -> 304 us (0.65)
  the two profiles are of different devices: /device:TPU:22 before, /device:TPU:0 now
where the time goes in v2:
time: 304 us
  Pallas kernels  276 us (91%)
  other arithmetic  10.5 us (3%)
  local copies, waits for them, and re-layouts  9.5 us (3%)
  between operations  8.09 us (3%)
    pallas_call x1, Pallas kernels, fused(): pl.pallas_call(fused_kernel, out_shape=jax.ShapeDtypeStruct((ROUNDS * row...  276 us
    convert_element_type x1, local copies, waits for them, and re-layouts, local(): spread = (table.T[None, :, :, None] * jnp.eye(GROUP, dtype=F32)[:, None,...  8.83 us

profile of v2, /device:TPU:0, one launch (start us, length us, event | category | flops | bytes accessed | tf_op | source)
XLA Modules:
  0.0 303.6 jit_solution(1817040456094488014)
XLA Ops:
  0.0 0.9 select_reduce_fusion.1
  1.0 0.2 convert_reduce_fusion
  1.2 0.1 select_reduce_fusion
  1.3 0.5 iota_subtract_fusion.pick_ref
  1.8 0.1 fusion.1
  1.9 0.1 fusion
  2.0 3.2 %multiply_convert_fusion = bf16[16,16,64,16]{3,2,1,0:T(8,128)(2,1)} fusion(f32[16,16]{1,0:T(8,128)S(1)} %fusion.2, f32[16,64]{1,0:T(8,128)S(1)} %fusion), kind=kLoop, calls=%fused_computation | loop fusion | flops 524288 | bytes 529408 | tf_op jit(solution)/shard_map/convert_element_type | solution.py:461
  5.1 8.8 %convert_element_type.28.table_ref = bf16[256,1024]{1,0:T(8,128)(2,1)} reshape(bf16[16,16,64,16]{3,2,1,0:T(8,128)(2,1)} %multiply_convert_fusion) | data formatting | bytes 1048576 | tf_op jit(solution)/shard_map/convert_element_type | solution.py:461
  14.0 275.5 %fused.1 = f32[4096,256]{1,0:T(8,128)} custom-call(s32[4]{0:T(128)} %iota_subtract_fusion.pick_ref, bf16[32,2,96,256]{3,2,1,0:T(8,128)(2,1)} %spec_ref.1, s32[1,256]{1,0:T(1,128)} %order_ref.1, bf16[256,1024]{1,0:T(8,128)(2,1)} %convert_element_type.28.table_ref), custom_call_target="tpu_custom_call" | custom-call | flops 16000000000 | bytes 16000000 | tf_op jit(solution)/shard_map/fused/pallas_call | solution.py:422
  289.5 0.0 copy-start
  289.5 0.7 fusion.6
  294.5 2.4 select_select_fusion.3
  300.7 0.0 copy-done
  300.7 0.3 select_select_fusion.1
  300.9 2.7 maximum_bitcast_fusion
  (4 shorter events, 0.1 us)
Async XLA Ops:
  289.5 11.2 %copy-start = (f32[4096,256]{1,0:T(8,128)S(1)}, f32[4096,256]{1,0:T(8,128)}, u32[]{:S(2)}) copy-start(f32[4096,256]{1,0:T(8,128)} %fused.1) | copy-start | bytes 12582916

commit v3 on v2

--- a/solution.py
+++ b/solution.py
@@ -2,6 +2,8 @@
 
 import jax
 import jax.numpy as jnp
+import ml_dtypes
+import numpy as np
 from jax import lax
 from jax.experimental import pallas as pl
 from jax.experimental.pallas import tpu as pltpu
@@ -15,11 +17,13 @@
 
 
 def make_table(num_bins, num_lags, window_total):
-    bin_freq = jnp.arange(num_bins, dtype=F32)[:, None]
-    lag_index = (jnp.arange(num_lags, dtype=jnp.int32) - num_lags // 2).astype(F32)[None, :]
+    bin_freq = np.arange(num_bins, dtype=np.float64)[:, None]
+    lag_index = (np.arange(num_lags) - num_lags // 2).astype(np.float64)[None, :]
     phase_angle = math.pi * bin_freq * lag_index / num_bins
     norm_factor = 1.0 / math.sqrt(window_total * num_bins)
-    return jnp.concatenate([jnp.cos(phase_angle), -jnp.sin(phase_angle)], 0) * norm_factor
+    table = np.concatenate([np.cos(phase_angle), -np.sin(phase_angle)], 0) * norm_factor
+    spread = table.T[None, :, :, None] * np.eye(GROUP)[:, None, None, :]
+    return spread.reshape(GROUP * num_lags, 2 * num_bins * GROUP).astype(ml_dtypes.bfloat16)
 
 
 def whiten_kernel(spec_ref, order_ref, own_ref, lhs_ref, power):
@@ -312,7 +316,7 @@
         return carry
 
     for h in range(HALVES):
-        lax.fori_loop(h * part, (h + 1) * part, scale, 0)
+        lax.fori_loop(h * part, (h + 1) * part, scale, 0, unroll=2)
         links(0, h)
 
     def turn_bin(f, carry):
@@ -323,7 +327,7 @@
         lhs[f] = turned.astype(BF)
         return carry
 
-    lax.fori_loop(0, nf, turn_bin, 0)
+    lax.fori_loop(0, nf, turn_bin, 0, unroll=4)
 
     def to_core(k):
         return pltpu.make_async_remote_copy(
@@ -360,7 +364,7 @@
             cross[nf + f] = jnp.dot(left, turned, preferred_element_type=F32).astype(BF)
             return carry
 
-        lax.fori_loop(0, nf, one_bin, 0)
+        lax.fori_loop(0, nf, one_bin, 0, unroll=4)
         if k >= 2:
             to_core(k - 2).wait_send()
 
@@ -385,9 +389,9 @@
             out_ref[pl.ds(to, size)] = lags_of(0, 0, u)
             return carry
 
-        lax.fori_loop(0, share // GROUP, send_group, 0)
+        lax.fori_loop(0, share // GROUP, send_group, 0, unroll=2)
         to_core(k).start()
-        lax.fori_loop(0, share // GROUP, keep_group, 0)
+        lax.fori_loop(0, share // GROUP, keep_group, 0, unroll=2)
         to_core(k).wait_recv()
         passed[k] = (keep[...] + beside[k, pl.ds(lag_rows, lag_rows)].astype(F32)).astype(BF)
         to_row(k).start()
@@ -451,14 +455,33 @@
     )(pick, spectra, order, table)
 
 
+def arrange_kernel(place_ref, sums_ref, out_ref):
+    out_ref[:, 0] = sums_ref[0]
+
+
+def arrange(place, sums):
+    rounds, rows, lags, nc = sums.shape
+    part = rows // 2
+    return pl.pallas_call(
+        arrange_kernel,
+        grid_spec=pltpu.PrefetchScalarGridSpec(
+            num_scalar_prefetch=1,
+            grid=(rounds, 2),
+            in_specs=[
+                pl.BlockSpec((1, part, lags, nc), lambda r, h, place: (place[r], h, 0, 0))
+            ],
+            out_specs=pl.BlockSpec((part, 1, lags, nc), lambda r, h, place: (h, r, 0, 0)),
+        ),
+        out_shape=jax.ShapeDtypeStruct((rows, rounds, lags, nc), F32),
+        name="arrange",
+    )(place, sums)
+
+
 def local(spectra, channel_order, partners):
     num_blocks = lax.axis_size("pair")
     win_count = lax.axis_size("win")
     nf, _, nw, nc = spectra.shape
-    table = make_table(nf, LAGS, nw * win_count)
-    spread = (
-        table.T[None, :, :, None] * jnp.eye(GROUP, dtype=F32)[:, None, None, :]
-    ).reshape(GROUP * LAGS, 2 * nf * GROUP).astype(BF)
+    spread = jnp.asarray(make_table(nf, LAGS, nw * win_count))
     me = lax.axis_index("pair")
     win = lax.axis_index("win")
     if num_blocks == 2 * CHAIN and win_count == 4:
@@ -472,14 +495,7 @@
         turns = jnp.arange(ROUNDS, dtype=jnp.int32)
         pick = jnp.sum(jnp.where(place[None, :] == turns[:, None], rank[None, :], 0), 1) - turns
         sums = fused(pick.astype(jnp.int32), spectra, channel_order, spread)
-        sums = sums.reshape(ROUNDS, nc // 4, LAGS, nc)
-        ordered = []
-        for turn in range(ROUNDS):
-            value = sums[ROUNDS - 1]
-            for k in range(ROUNDS - 1):
-                value = jnp.where(place[turn] == k, sums[k], value)
-            ordered.append(value)
-        return jnp.stack(ordered, 1)[None]
+        return arrange(place, sums.reshape(ROUNDS, nc // 4, LAGS, nc))[None]
     own, lhs = whiten(spectra, channel_order)
     row, core = win // 2, win % 2
     results = []

time: 304 us -> 279 us (0.918)
  local copies, waits for them, and re-layouts: 9.5 us -> 0.01 us
  other arithmetic: 10.5 us -> 1.78 us
  between operations: 8.09 us -> 0.03 us
    convert_element_type x1 -> x0, local copies, waits for them, and re-layouts: 8.83 us -> none  [local(): spread = (table.T[None, :, :, None] * jnp.eye(GROUP, dtype=F32)[:, None,...]
    pallas_call x0 -> x1, Pallas kernels: none -> 7.28 us  [arrange(): pl.pallas_call(arrange_kernel, grid_spec=pltpu.PrefetchScalarGridSpec(num...]
    pallas_call x1, Pallas kernels: 276 us -> 269 us  [fused(): pl.pallas_call(fused_kernel, out_shape=jax.ShapeDtypeStruct((ROUNDS * row...]
    convert_element_type x3 -> x0, other arithmetic: 3.16 us -> none  [the longest x1 3.15 us: local(): spread = (table.T[None, :, :, None] * jnp.eye(GROUP, dtype=F32)[:, None,...]
where the time goes in v3:
time: 279 us; the launch traced here: 278 us
  Pallas kernels  277 us (99%)
    pallas_call x1, Pallas kernels, fused(): pl.pallas_call(fused_kernel, out_shape=jax.ShapeDtypeStruct((ROUNDS * row...  269 us
    pallas_call x1, Pallas kernels, arrange(): pl.pallas_call(arrange_kernel, grid_spec=pltpu.PrefetchScalarGridSpec(num...  7.28 us

profile of v3, /device:TPU:0, one launch (start us, length us, event | category | flops | bytes accessed | tf_op | source)
XLA Modules:
  0.0 278.3 jit_solution(5721498584333145404)
XLA Ops:
  0.0 0.9 select_reduce_fusion.1
  1.0 0.2 convert_reduce_fusion.place_ref
  1.2 0.0 copy-start
  1.2 0.1 select_reduce_fusion
  1.3 0.5 iota_subtract_fusion.pick_ref
  1.8 269.2 %fused.1 = f32[4096,256]{1,0:T(8,128)} custom-call(s32[4]{0:T(128)} %iota_subtract_fusion.pick_ref, bf16[32,2,96,256]{3,2,1,0:T(8,128)(2,1)} %spec_ref.1, s32[1,256]{1,0:T(1,128)} %order_ref.1, bf16[256,1024]{1,0:T(8,128)(2,1)} %constant.312.clone.table_ref), custom_call_target="tpu_custom_call" | custom-call | flops 16000000000 | bytes 16000000 | tf_op jit(solution)/shard_map/fused/pallas_call | solution.py:426
  271.0 0.0 copy-done
  271.1 7.3 %arrange.1 = f32[64,4,16,256]{3,2,1,0:T(8,128)} custom-call(s32[4]{0:T(128)} %copy-done, f32[4,64,16,256]{3,2,1,0:T(8,128)} %bitcast.2), custom_call_target="tpu_custom_call" | custom-call | tf_op jit(solution)/shard_map/arrange/pallas_call | solution.py:465
  (1 shorter events, 0.0 us)
Async XLA Ops:
  1.2 269.9 %copy-start = (s32[4]{0:T(128)}, s32[4]{0:T(128)S(1)}, u32[]{:S(2)}) copy-start(s32[4]{0:T(128)S(1)} %convert_reduce_fusion.place_ref) | copy-start | bytes 52

commit v4 on v3

--- a/solution.py
+++ b/solution.py
@@ -1,3 +1,4 @@
+import functools
 import math
 
 import jax
@@ -38,7 +39,7 @@
         power[f + 2] = re * re + im * im
         return carry
 
-    lax.fori_loop(0, nf, square, 0)
+    lax.fori_loop(0, nf, square, 0, unroll=4)
     rows = lax.broadcasted_iota(jnp.int32, (nc, nc), 0)
     cols = lax.broadcasted_iota(jnp.int32, (nc, nc), 1)
     pick = (rows == order_ref[...]).astype(F32).astype(BF)
@@ -215,7 +216,7 @@
 
 def fused_kernel(
     pick_ref, spec_ref, order_ref, table_ref, out_ref,
-    blocks, lhs, cross, keep, give, beside, passed, across,
+    blocks, lhs, cross, perm, keep, give, beside, passed, across,
     swap_sem, chain_sem, got_sem, give_sem, beside_sem, passed_sem, across_sem,
 ):
     nf, _, nw, nc = spec_ref.shape
@@ -249,13 +250,14 @@
     def _():
         signal({"pair": pair + 2})
 
-    @pl.when((c > 0) & (c < CHAIN - 1))
-    def _():
-        pl.semaphore_wait(pltpu.get_barrier_semaphore(), 5)
-
-    @pl.when((c == 0) | (c == CHAIN - 1))
-    def _():
-        pl.semaphore_wait(pltpu.get_barrier_semaphore(), 4)
+    def greet():
+        @pl.when((c > 0) & (c < CHAIN - 1))
+        def _():
+            pl.semaphore_wait(pltpu.get_barrier_semaphore(), 5)
+
+        @pl.when((c == 0) | (c == CHAIN - 1))
+        def _():
+            pl.semaphore_wait(pltpu.get_barrier_semaphore(), 4)
 
     def copy(way, item):
         b, sw, h = item
@@ -293,12 +295,13 @@
     zero = jnp.zeros((nw, nc), F32)
     for edge in (0, 1, nf + 2, nf + 3):
         out_ref[pl.ds(edge * nw, nw)] = zero
-    lax.fori_loop(0, nf, square, 0)
+    lax.fori_loop(0, nf, square, 0, unroll=4)
     rows = lax.broadcasted_iota(jnp.int32, (nc, nc), 0)
     cols = lax.broadcasted_iota(jnp.int32, (nc, nc), 1)
+    perm[0] = (rows == order_ref[...]).astype(F32).astype(BF)
+    perm[1] = (rows == cols).astype(F32).astype(BF)
 
     def scale(f, carry):
-        pick = (rows == order_ref[...]).astype(F32).astype(BF)
         total = out_ref[pl.ds(pl.multiple_of(f * nw, 8), nw)]
         for d in range(1, 5):
             total += out_ref[pl.ds(pl.multiple_of((f + d) * nw, 8), nw)]
@@ -312,28 +315,29 @@
             ],
             0,
         )
-        blocks[pair, f] = jnp.dot(white, pick, preferred_element_type=F32).astype(BF)
-        return carry
-
+        blocks[pair, f] = jnp.dot(white, perm[0], preferred_element_type=F32).astype(BF)
+        return carry
+
+    greet()
     for h in range(HALVES):
-        lax.fori_loop(h * part, (h + 1) * part, scale, 0, unroll=2)
+        lax.fori_loop(h * part, (h + 1) * part, scale, 0, unroll=4)
         links(0, h)
 
     def turn_bin(f, carry):
-        eye = (rows == cols).astype(F32).astype(BF)
         turned = lax.dot_general(
-            eye, blocks[pair, f], (((1,), (1,)), ((), ())), preferred_element_type=F32
+            perm[1], blocks[pair, f], (((1,), (1,)), ((), ())), preferred_element_type=F32
         )
         lhs[f] = turned.astype(BF)
         return carry
 
     lax.fori_loop(0, nf, turn_bin, 0, unroll=4)
 
-    def to_core(k):
+    def to_core(k, half):
+        at = pl.ds(half * lag_rows, lag_rows)
         return pltpu.make_async_remote_copy(
-            src_ref=give.at[k % 2], dst_ref=beside.at[k], send_sem=give_sem.at[k],
-            recv_sem=beside_sem.at[k], device_id=core_to,
-            device_id_type=pl.DeviceIdType.MESH,
+            src_ref=give.at[k % 2, at], dst_ref=beside.at[k, at],
+            send_sem=give_sem.at[k, half], recv_sem=beside_sem.at[k, half],
+            device_id=core_to, device_id_type=pl.DeviceIdType.MESH,
         )
 
     def to_row(k):
@@ -366,7 +370,8 @@
 
         lax.fori_loop(0, nf, one_bin, 0, unroll=4)
         if k >= 2:
-            to_core(k - 2).wait_send()
+            for half in range(2):
+                to_core(k - 2, half).wait_send()
 
         def lags_of(half, other, u):
             owner = lax.rem(row + half, 2) * 2 + lax.rem(core + other, 2)
@@ -376,26 +381,31 @@
 
         size = GROUP * LAGS
 
-        def send_group(u, carry):
-            for half in range(2):
-                at = pl.multiple_of(half * lag_rows + u * size, size)
-                give[k % 2, pl.ds(at, size)] = lags_of(half, 1, u).astype(BF)
+        def send_group(half, u, carry):
+            at = pl.multiple_of(half * lag_rows + u * size, size)
+            give[k % 2, pl.ds(at, size)] = lags_of(half, 1, u).astype(BF)
             return carry
 
-        def keep_group(u, carry):
-            at = pl.multiple_of(u * size, size)
-            keep[pl.ds(at, size)] = lags_of(1, 0, u)
-            to = pl.multiple_of(k * lag_rows + u * size, size)
-            out_ref[pl.ds(to, size)] = lags_of(0, 0, u)
+        def keep_group(half, u, carry):
+            if half == 1:
+                keep[pl.ds(pl.multiple_of(u * size, size), size)] = lags_of(1, 0, u)
+            else:
+                to = pl.multiple_of(k * lag_rows + u * size, size)
+                out_ref[pl.ds(to, size)] = lags_of(0, 0, u)
             return carry
 
-        lax.fori_loop(0, share // GROUP, send_group, 0, unroll=2)
-        to_core(k).start()
-        lax.fori_loop(0, share // GROUP, keep_group, 0, unroll=2)
-        to_core(k).wait_recv()
-        passed[k] = (keep[...] + beside[k, pl.ds(lag_rows, lag_rows)].astype(F32)).astype(BF)
-        to_row(k).start()
-        out_ref[pl.ds(k * lag_rows, lag_rows)] += beside[k, pl.ds(0, lag_rows)].astype(F32)
+        groups = share // GROUP
+        for half in (1, 0):
+            lax.fori_loop(0, groups, functools.partial(send_group, half), 0, unroll=2)
+            to_core(k, half).start()
+            lax.fori_loop(0, groups, functools.partial(keep_group, half), 0, unroll=2)
+            to_core(k, half).wait_recv()
+            got = beside[k, pl.ds(half * lag_rows, lag_rows)].astype(F32)
+            if half == 1:
+                passed[k] = (keep[...] + got).astype(BF)
+                to_row(k).start()
+            else:
+                out_ref[pl.ds(k * lag_rows, lag_rows)] += got
 
     for t in range(1, STEPS):
         links(t)
@@ -406,7 +416,8 @@
         out_ref[pl.ds(k * lag_rows, lag_rows)] += across[k].astype(F32)
     for k in range(ROUNDS):
         if k >= 2:
-            to_core(k).wait_send()
+            for half in range(2):
+                to_core(k, half).wait_send()
         to_row(k).wait_send()
     for cs in range(CHAIN):
 
@@ -432,6 +443,7 @@
             pltpu.VMEM((blocks, nf, 2 * nw, nc), BF),
             pltpu.VMEM((nf, nc, 2 * nw), BF),
             pltpu.VMEM((2 * nf, nc, nc), BF),
+            pltpu.VMEM((2, nc, nc), BF),
             pltpu.VMEM((rows, nc), F32),
             pltpu.VMEM((2, 2 * rows, nc), BF),
             pltpu.VMEM((ROUNDS, 2 * rows, nc), BF),
@@ -440,8 +452,8 @@
             dma((CHAIN, HALVES)),
             dma((2, 2 * CHAIN, HALVES)),
             dma((blocks, HALVES)),
-            dma((ROUNDS,)),
-            dma((ROUNDS,)),
+            dma((ROUNDS, 2)),
+            dma((ROUNDS, 2)),
             dma((ROUNDS,)),
             dma((ROUNDS,)),
         ],
@@ -455,24 +467,29 @@
     )(pick, spectra, order, table)
 
 
-def arrange_kernel(place_ref, sums_ref, out_ref):
-    out_ref[:, 0] = sums_ref[0]
+def arrange_kernel(place_ref, sums_ref, out_ref, sem):
+    rounds = sums_ref.shape[0]
+    copies = [
+        pltpu.make_async_copy(sums_ref.at[place_ref[r]], out_ref.at[:, r], sem.at[r])
+        for r in range(rounds)
+    ]
+    for copy in copies:
+        copy.start()
+    for copy in copies:
+        copy.wait()
 
 
 def arrange(place, sums):
     rounds, rows, lags, nc = sums.shape
-    part = rows // 2
     return pl.pallas_call(
         arrange_kernel,
-        grid_spec=pltpu.PrefetchScalarGridSpec(
-            num_scalar_prefetch=1,
-            grid=(rounds, 2),
-            in_specs=[
-                pl.BlockSpec((1, part, lags, nc), lambda r, h, place: (place[r], h, 0, 0))
-            ],
-            out_specs=pl.BlockSpec((part, 1, lags, nc), lambda r, h, place: (h, r, 0, 0)),
-        ),
+        in_specs=[
+            pl.BlockSpec(memory_space=pltpu.SMEM),
+            pl.BlockSpec(memory_space=pl.ANY),
+        ],
+        out_specs=pl.BlockSpec(memory_space=pl.ANY),
         out_shape=jax.ShapeDtypeStruct((rows, rounds, lags, nc), F32),
+        scratch_shapes=[pltpu.SemaphoreType.DMA((rounds,))],
         name="arrange",
     )(place, sums)
 

time: 279 us -> 398 us (1.43)
  Pallas kernels: 277 us -> 396 us
    pallas_call x1, Pallas kernels: 7.28 us -> 129 us  [arrange(): pl.pallas_call(arrange_kernel, in_specs=[pl.BlockSpec(memory_space=pltpu....]
where the time goes in v4:
time: 398 us
  Pallas kernels  396 us (99%)
    pallas_call x1, Pallas kernels, fused(): pl.pallas_call(fused_kernel, out_shape=jax.ShapeDtypeStruct((ROUNDS * row...  267 us
    pallas_call x1, Pallas kernels, arrange(): pl.pallas_call(arrange_kernel, in_specs=[pl.BlockSpec(memory_space=pltpu....  129 us

profile of v4, /device:TPU:0, one launch (start us, length us, event | category | flops | bytes accessed | tf_op | source)
XLA Modules:
  0.0 397.7 jit_solution(9482226801959972621)
XLA Ops:
  0.0 0.9 select_reduce_fusion.1
  1.0 0.2 convert_reduce_fusion.place_ref
  1.2 0.0 copy-start
  1.2 0.1 select_reduce_fusion
  1.3 0.5 iota_subtract_fusion.pick_ref
  1.8 267.1 %fused.1 = f32[4096,256]{1,0:T(8,128)} custom-call(s32[4]{0:T(128)} %iota_subtract_fusion.pick_ref, bf16[32,2,96,256]{3,2,1,0:T(8,128)(2,1)} %spec_ref.1, s32[1,256]{1,0:T(1,128)} %order_ref.1, bf16[256,1024]{1,0:T(8,128)(2,1)} %constant.312.clone.table_ref), custom_call_target="tpu_custom_call" | custom-call | flops 16000000000 | bytes 16000000 | tf_op jit(solution)/shard_map/fused/pallas_call | solution.py:437
  268.9 0.0 copy-done
  268.9 128.9 %arrange.1 = f32[64,4,16,256]{3,2,1,0:T(8,128)} custom-call(s32[4]{0:T(128)} %copy-done, f32[4,64,16,256]{3,2,1,0:T(8,128)} %bitcast.2), custom_call_target="tpu_custom_call" | custom-call | tf_op jit(solution)/shard_map/arrange/pallas_call | solution.py:484
  (1 shorter events, 0.0 us)
Async XLA Ops:
  1.2 267.7 %copy-start = (s32[4]{0:T(128)}, s32[4]{0:T(128)S(1)}, u32[]{:S(2)}) copy-start(s32[4]{0:T(128)S(1)} %convert_reduce_fusion.place_ref) | copy-start | bytes 52

commit v5 on v4

--- a/solution.py
+++ b/solution.py
@@ -149,23 +149,25 @@
 
 
 CHAIN = 4
-HALVES = 2
+PARTS = 4
+AHEAD = 2
 ARRIVAL = (
     ((0, 1), (1, 0), (1, 1), (2, 0), (3, 0), (2, 1), (3, 1)),
     ((1, 1), (0, 0), (2, 0), (0, 1), (3, 0), (2, 1), (3, 1)),
     ((2, 1), (3, 0), (1, 0), (3, 1), (0, 0), (1, 1), (0, 1)),
     ((3, 1), (2, 0), (2, 1), (1, 0), (0, 0), (1, 1), (0, 1)),
 )
-STEPS = 8
-TURN_AFTER = {4: (0,), 6: (1, 2), 7: (3,)}
+STEPS = 15
+TURN_AFTER = {8: (0,), 12: (1, 2), 14: (3,)}
+EARLY, EARLY_STEP = (0, 2), 13
 
 
 def plan_links():
     last = CHAIN - 1
     queue = {}
     for c in range(CHAIN):
-        down = [(b, 0, h) for b in range(c, CHAIN) for h in range(HALVES)] + [(last, 1, 1)]
-        up = [(b, 0, h) for b in range(c, -1, -1) for h in range(HALVES)] + [(0, 1, 1)]
+        down = [(b, 0, h) for b in range(c, CHAIN) for h in range(PARTS)] + [(last, 1, h) for h in (2, 3)]
+        up = [(b, 0, h) for b in range(c, -1, -1) for h in range(PARTS)] + [(0, 1, h) for h in (2, 3)]
         if c > 0:
             queue[c, "down"] = down
         if c < last:
@@ -175,12 +177,12 @@
             near = [0, 2, 3]
         if c == 2:
             near = [3, 1, 0]
-        swap = [(c, 0, 0), (c, 0, 1)]
+        swap = [(c, 0, h) for h in range(PARTS)]
         for b in near:
             by_chain = (b == last and c < last) or (b == 0 and c > 0)
-            swap += [(b, 0, h) for h in range(HALVES) if not (by_chain and h == 1)]
+            swap += [(b, 0, h) for h in range(PARTS) if not (by_chain and h >= 2)]
         queue[c, "swap"] = swap
-    have = {(c, (c, 0, h)): 0 for c in range(CHAIN) for h in range(HALVES)}
+    have = {(c, (c, 0, h)): 0 for c in range(CHAIN) for h in range(PARTS)}
     start = {key: [] for key in queue}
     for t in range(STEPS):
         new = {}
@@ -204,13 +206,14 @@
     for (c, way), items in queue.items():
         assert len(start[c, way]) == len(items)
         for item, t in zip(items, start[c, way]):
-            sends[c, max(t - 1, have[c, item], 0)].append((way, item))
+            sends[c, max(t - AHEAD, have[c, item], 0)].append((way, item))
     for c in range(CHAIN):
         for k in range(ROUNDS):
             step = [t for t, turns in TURN_AFTER.items() if k in turns][0]
             for b, sw in ARRIVAL[c][k : k + 4]:
-                for h in range(HALVES):
-                    assert have[c, (b, sw, h)] <= step
+                for h in range(PARTS):
+                    early = k == ROUNDS - 1 and h in EARLY
+                    assert have[c, (b, sw, h)] <= (EARLY_STEP if early else step)
     return waits, sends
 
 
@@ -220,7 +223,7 @@
     swap_sem, chain_sem, got_sem, give_sem, beside_sem, passed_sem, across_sem,
 ):
     nf, _, nw, nc = spec_ref.shape
-    part = nf // HALVES
+    part = nf // PARTS
     share = nc // 4
     lag_rows = share * LAGS
     pair = lax.axis_index("pair")
@@ -319,7 +322,7 @@
         return carry
 
     greet()
-    for h in range(HALVES):
+    for h in range(PARTS):
         lax.fori_loop(h * part, (h + 1) * part, scale, 0, unroll=4)
         links(0, h)
 
@@ -347,7 +350,7 @@
             device_id_type=pl.DeviceIdType.MESH,
         )
 
-    def correlate_turn(k):
+    def cross_turn(k, parts):
         places = []
         for m in range(4):
             at = jnp.int32(0)
@@ -368,7 +371,10 @@
             cross[nf + f] = jnp.dot(left, turned, preferred_element_type=F32).astype(BF)
             return carry
 
-        lax.fori_loop(0, nf, one_bin, 0, unroll=4)
+        for h in parts:
+            lax.fori_loop(h * part, (h + 1) * part, one_bin, 0, unroll=4)
+
+    def lag_turn(k):
         if k >= 2:
             for half in range(2):
                 to_core(k - 2, half).wait_send()
@@ -410,7 +416,11 @@
     for t in range(1, STEPS):
         links(t)
         for k in TURN_AFTER.get(t, ()):
-            correlate_turn(k)
+            late = k == ROUNDS - 1
+            cross_turn(k, [h for h in range(PARTS) if not (late and h in EARLY)])
+            lag_turn(k)
+        if t == EARLY_STEP:
+            cross_turn(ROUNDS - 1, EARLY)
     for k in range(ROUNDS):
         to_row(k).wait_recv()
         out_ref[pl.ds(k * lag_rows, lag_rows)] += across[k].astype(F32)
@@ -449,9 +459,9 @@
             pltpu.VMEM((ROUNDS, 2 * rows, nc), BF),
             pltpu.VMEM((ROUNDS, rows, nc), BF),
             pltpu.VMEM((ROUNDS, rows, nc), BF),
-            dma((CHAIN, HALVES)),
-            dma((2, 2 * CHAIN, HALVES)),
-            dma((blocks, HALVES)),
+            dma((CHAIN, PARTS)),
+            dma((2, 2 * CHAIN, PARTS)),
+            dma((blocks, PARTS)),
             dma((ROUNDS, 2)),
             dma((ROUNDS, 2)),
             dma((ROUNDS,)),
@@ -467,16 +477,27 @@
     )(pick, spectra, order, table)
 
 
-def arrange_kernel(place_ref, sums_ref, out_ref, sem):
-    rounds = sums_ref.shape[0]
-    copies = [
-        pltpu.make_async_copy(sums_ref.at[place_ref[r]], out_ref.at[:, r], sem.at[r])
-        for r in range(rounds)
-    ]
-    for copy in copies:
-        copy.start()
-    for copy in copies:
-        copy.wait()
+def arrange_kernel(place_ref, sums_ref, out_ref, held, in_sem, out_sem):
+    rounds, rows = held.shape[:2]
+    half = rows // 2
+    for r in range(rounds):
+        for h in range(2):
+            at = pl.ds(h * half, half)
+            pltpu.make_async_copy(
+                sums_ref.at[place_ref[r], at], held.at[r, at], in_sem.at[r, h]
+            ).start()
+    for step in ("move", "finish"):
+        for r in range(rounds):
+            for h in range(2):
+                at = pl.ds(h * half, half)
+                out = pltpu.make_async_copy(held.at[r, at], out_ref.at[at, r], out_sem.at[r, h])
+                if step == "move":
+                    pltpu.make_async_copy(
+                        sums_ref.at[place_ref[r], at], held.at[r, at], in_sem.at[r, h]
+                    ).wait()
+                    out.start()
+                else:
+                    out.wait()
 
 
 def arrange(place, sums):
@@ -489,7 +510,11 @@
         ],
         out_specs=pl.BlockSpec(memory_space=pl.ANY),
         out_shape=jax.ShapeDtypeStruct((rows, rounds, lags, nc), F32),
-        scratch_shapes=[pltpu.SemaphoreType.DMA((rounds,))],
+        scratch_shapes=[
+            pltpu.VMEM((rounds, rows, lags, nc), F32),
+            pltpu.SemaphoreType.DMA((rounds, 2)),
+            pltpu.SemaphoreType.DMA((rounds, 2)),
+        ],
         name="arrange",
     )(place, sums)
 

time: 398 us -> 271 us (0.68)
  Pallas kernels: 396 us -> 269 us
    pallas_call x1, Pallas kernels: 129 us -> 4.24 us  [arrange(): pl.pallas_call(arrange_kernel, in_specs=[pl.BlockSpec(memory_space=pltpu....]
where the time goes in v5:
time: 271 us
  Pallas kernels  269 us (99%)
    pallas_call x1, Pallas kernels, fused(): pl.pallas_call(fused_kernel, out_shape=jax.ShapeDtypeStruct((ROUNDS * row...  265 us

profile of v5, /device:TPU:0, one launch (start us, length us, event | category | flops | bytes accessed | tf_op | source)
XLA Modules:
  0.0 271.2 jit_solution(10818844876276482199)
XLA Ops:
  0.0 0.9 select_reduce_fusion.1
  1.0 0.2 convert_reduce_fusion.place_ref
  1.2 0.0 copy-start
  1.2 0.1 select_reduce_fusion
  1.3 0.5 iota_subtract_fusion.pick_ref
  1.8 265.0 %fused.1 = f32[4096,256]{1,0:T(8,128)} custom-call(s32[4]{0:T(128)} %iota_subtract_fusion.pick_ref, bf16[32,2,96,256]{3,2,1,0:T(8,128)(2,1)} %spec_ref.1, s32[1,256]{1,0:T(1,128)} %order_ref.1, bf16[256,1024]{1,0:T(8,128)(2,1)} %constant.312.clone.table_ref), custom_call_target="tpu_custom_call" | custom-call | flops 16000000000 | bytes 16000000 | tf_op jit(solution)/shard_map/fused/pallas_call | solution.py:447
  266.8 0.0 copy-done
  266.8 4.2 %arrange.1 = f32[64,4,16,256]{3,2,1,0:T(8,128)} custom-call(s32[4]{0:T(128)} %copy-done, f32[4,64,16,256]{3,2,1,0:T(8,128)} %bitcast.2), custom_call_target="tpu_custom_call" | custom-call | tf_op jit(solution)/shard_map/arrange/pallas_call | solution.py:505
  (1 shorter events, 0.0 us)
Async XLA Ops:
  1.2 265.6 %copy-start = (s32[4]{0:T(128)}, s32[4]{0:T(128)S(1)}, u32[]{:S(2)}) copy-start(s32[4]{0:T(128)S(1)} %convert_reduce_fusion.place_ref) | copy-start | bytes 52

commit v6 on v5

--- a/solution.py
+++ b/solution.py
@@ -298,7 +298,7 @@
     zero = jnp.zeros((nw, nc), F32)
     for edge in (0, 1, nf + 2, nf + 3):
         out_ref[pl.ds(edge * nw, nw)] = zero
-    lax.fori_loop(0, nf, square, 0, unroll=4)
+    lax.fori_loop(0, part + 2, square, 0, unroll=5)
     rows = lax.broadcasted_iota(jnp.int32, (nc, nc), 0)
     cols = lax.broadcasted_iota(jnp.int32, (nc, nc), 1)
     perm[0] = (rows == order_ref[...]).astype(F32).astype(BF)
@@ -325,6 +325,8 @@
     for h in range(PARTS):
         lax.fori_loop(h * part, (h + 1) * part, scale, 0, unroll=4)
         links(0, h)
+        if h == 0:
+            lax.fori_loop(part + 2, nf, square, 0, unroll=2)
 
     def turn_bin(f, carry):
         turned = lax.dot_general(
@@ -335,19 +337,22 @@
 
     lax.fori_loop(0, nf, turn_bin, 0, unroll=4)
 
-    def to_core(k, half):
-        at = pl.ds(half * lag_rows, lag_rows)
+    piece_rows = lag_rows // 2
+
+    def to_core(k, half, piece):
+        at = pl.ds(half * lag_rows + piece * piece_rows, piece_rows)
         return pltpu.make_async_remote_copy(
             src_ref=give.at[k % 2, at], dst_ref=beside.at[k, at],
-            send_sem=give_sem.at[k, half], recv_sem=beside_sem.at[k, half],
+            send_sem=give_sem.at[k, half, piece], recv_sem=beside_sem.at[k, half, piece],
             device_id=core_to, device_id_type=pl.DeviceIdType.MESH,
         )
 
-    def to_row(k):
+    def to_row(k, piece):
+        at = pl.ds(piece * piece_rows, piece_rows)
         return pltpu.make_async_remote_copy(
-            src_ref=passed.at[k], dst_ref=across.at[k], send_sem=passed_sem.at[k],
-            recv_sem=across_sem.at[k], device_id=row_to,
-            device_id_type=pl.DeviceIdType.MESH,
+            src_ref=passed.at[k, at], dst_ref=across.at[k, at],
+            send_sem=passed_sem.at[k, piece], recv_sem=across_sem.at[k, piece],
+            device_id=row_to, device_id_type=pl.DeviceIdType.MESH,
         )
 
     def cross_turn(k, parts):
@@ -377,7 +382,8 @@
     def lag_turn(k):
         if k >= 2:
             for half in range(2):
-                to_core(k - 2, half).wait_send()
+                for piece in range(2):
+                    to_core(k - 2, half, piece).wait_send()
 
         def lags_of(half, other, u):
             owner = lax.rem(row + half, 2) * 2 + lax.rem(core + other, 2)
@@ -400,18 +406,26 @@
                 out_ref[pl.ds(to, size)] = lags_of(0, 0, u)
             return carry
 
-        groups = share // GROUP
+        groups = share // GROUP // 2
+
+        def receive(half, piece):
+            to_core(k, half, piece).wait_recv()
+            at = half * lag_rows + piece * piece_rows
+            return beside[k, pl.ds(at, piece_rows)].astype(F32)
+
         for half in (1, 0):
-            lax.fori_loop(0, groups, functools.partial(send_group, half), 0, unroll=2)
-            to_core(k, half).start()
-            lax.fori_loop(0, groups, functools.partial(keep_group, half), 0, unroll=2)
-            to_core(k, half).wait_recv()
-            got = beside[k, pl.ds(half * lag_rows, lag_rows)].astype(F32)
-            if half == 1:
-                passed[k] = (keep[...] + got).astype(BF)
-                to_row(k).start()
-            else:
-                out_ref[pl.ds(k * lag_rows, lag_rows)] += got
+            for piece in range(2):
+                first, last = piece * groups, (piece + 1) * groups
+                lax.fori_loop(first, last, functools.partial(send_group, half), 0, unroll=2)
+                to_core(k, half, piece).start()
+                lax.fori_loop(first, last, functools.partial(keep_group, half), 0, unroll=2)
+                if half == 1:
+                    at = pl.ds(piece * piece_rows, piece_rows)
+                    passed[k, at] = (keep[at] + receive(half, piece)).astype(BF)
+                    to_row(k, piece).start()
+        for piece in range(2):
+            at = pl.ds(k * lag_rows + piece * piece_rows, piece_rows)
+            out_ref[at] += receive(0, piece)
 
     for t in range(1, STEPS):
         links(t)
@@ -422,13 +436,16 @@
         if t == EARLY_STEP:
             cross_turn(ROUNDS - 1, EARLY)
     for k in range(ROUNDS):
-        to_row(k).wait_recv()
-        out_ref[pl.ds(k * lag_rows, lag_rows)] += across[k].astype(F32)
+        for piece in range(2):
+            to_row(k, piece).wait_recv()
+            at = pl.ds(k * lag_rows + piece * piece_rows, piece_rows)
+            out_ref[at] += across[k, pl.ds(piece * piece_rows, piece_rows)].astype(F32)
     for k in range(ROUNDS):
-        if k >= 2:
-            for half in range(2):
-                to_core(k, half).wait_send()
-        to_row(k).wait_send()
+        for piece in range(2):
+            if k >= 2:
+                for half in range(2):
+                    to_core(k, half, piece).wait_send()
+            to_row(k, piece).wait_send()
     for cs in range(CHAIN):
 
         @pl.when(c == cs)
@@ -462,10 +479,10 @@
             dma((CHAIN, PARTS)),
             dma((2, 2 * CHAIN, PARTS)),
             dma((blocks, PARTS)),
+            dma((ROUNDS, 2, 2)),
+            dma((ROUNDS, 2, 2)),
             dma((ROUNDS, 2)),
             dma((ROUNDS, 2)),
-            dma((ROUNDS,)),
-            dma((ROUNDS,)),
         ],
         cost_estimate=pl.CostEstimate(
             flops=16_000_000_000, bytes_accessed=16_000_000, transcendentals=0

time: 271 us -> 271 us (level)
  no operation moved by 1% of the time
where the time goes in v6:
time: 271 us; the launch traced here: 270 us
  Pallas kernels  268 us (99%)
    pallas_call x1, Pallas kernels, fused(): pl.pallas_call(fused_kernel, out_shape=jax.ShapeDtypeStruct((ROUNDS * row...  264 us

profile of v6, /device:TPU:0, one launch (start us, length us, event | category | flops | bytes accessed | tf_op | source)
XLA Modules:
  0.0 270.4 jit_solution(13329452822361523827)
XLA Ops:
  0.0 0.9 select_reduce_fusion.1
  1.0 0.2 convert_reduce_fusion.place_ref
  1.2 0.0 copy-start
  1.2 0.1 select_reduce_fusion
  1.3 0.5 iota_subtract_fusion.pick_ref
  1.8 264.2 %fused.1 = f32[4096,256]{1,0:T(8,128)} custom-call(s32[4]{0:T(128)} %iota_subtract_fusion.pick_ref, bf16[32,2,96,256]{3,2,1,0:T(8,128)(2,1)} %spec_ref.1, s32[1,256]{1,0:T(1,128)} %order_ref.1, bf16[256,1024]{1,0:T(8,128)(2,1)} %constant.312.clone.table_ref), custom_call_target="tpu_custom_call" | custom-call | flops 16000000000 | bytes 16000000 | tf_op jit(solution)/shard_map/fused/pallas_call | solution.py:464
  266.0 0.0 copy-done
  266.0 4.2 %arrange.1 = f32[64,4,16,256]{3,2,1,0:T(8,128)} custom-call(s32[4]{0:T(128)} %copy-done, f32[4,64,16,256]{3,2,1,0:T(8,128)} %bitcast.2), custom_call_target="tpu_custom_call" | custom-call | tf_op jit(solution)/shard_map/arrange/pallas_call | solution.py:522
  (1 shorter events, 0.0 us)
Async XLA Ops:
  1.2 264.8 %copy-start = (s32[4]{0:T(128)}, s32[4]{0:T(128)S(1)}, u32[]{:S(2)}) copy-start(s32[4]{0:T(128)S(1)} %convert_reduce_fusion.place_ref) | copy-start | bytes 52

commit v7 on v6

--- a/solution.py
+++ b/solution.py
@@ -150,7 +150,6 @@
 
 CHAIN = 4
 PARTS = 4
-AHEAD = 2
 ARRIVAL = (
     ((0, 1), (1, 0), (1, 1), (2, 0), (3, 0), (2, 1), (3, 1)),
     ((1, 1), (0, 0), (2, 0), (0, 1), (3, 0), (2, 1), (3, 1)),
@@ -206,7 +205,9 @@
     for (c, way), items in queue.items():
         assert len(start[c, way]) == len(items)
         for item, t in zip(items, start[c, way]):
-            sends[c, max(t - AHEAD, have[c, item], 0)].append((way, item))
+            ahead = 2 if t < 10 else 1 if t < 12 else 0
+            assert have[c, item] < t or t < 12
+            sends[c, max(t - ahead, have[c, item], 0)].append((way, item))
     for c in range(CHAIN):
         for k in range(ROUNDS):
             step = [t for t, turns in TURN_AFTER.items() if k in turns][0]
@@ -277,15 +278,15 @@
             device_id=to, device_id_type=pl.DeviceIdType.MESH,
         )
 
-    def links(t, only=None):
+    def links(t, only=None, wait=True, start=True):
         for cs in range(CHAIN):
 
             @pl.when(c == cs)
             def _(cs=cs):
-                if only in (None, 0):
+                if wait and only in (None, 0):
                     for item in waits[cs, t]:
                         copy("swap", item).wait_recv()
-                for way, item in sends[cs, t]:
+                for way, item in sends[cs, t] if start else ():
                     if only is None or item[2] == only:
                         copy(way, item).start()
 
@@ -428,8 +429,10 @@
             out_ref[at] += receive(0, piece)
 
     for t in range(1, STEPS):
-        links(t)
+        links(t, start=t != EARLY_STEP)
         for k in TURN_AFTER.get(t, ()):
+            if k == 2:
+                links(EARLY_STEP, wait=False)
             late = k == ROUNDS - 1
             cross_turn(k, [h for h in range(PARTS) if not (late and h in EARLY)])
             lag_turn(k)

time: 271 us -> 272 us (level)
  no operation moved by 1% of the time
where the time goes in v7:
time: 272 us
  Pallas kernels  270 us (99%)
    pallas_call x1, Pallas kernels, fused(): pl.pallas_call(fused_kernel, out_shape=jax.ShapeDtypeStruct((ROUNDS * row...  266 us

profile of v7, /device:TPU:0, one launch (start us, length us, event | category | flops | bytes accessed | tf_op | source)
XLA Modules:
  0.0 271.7 jit_solution(3646129232745110256)
XLA Ops:
  0.0 0.9 select_reduce_fusion.1
  1.0 0.2 convert_reduce_fusion.place_ref
  1.2 0.0 copy-start
  1.2 0.1 select_reduce_fusion
  1.3 0.5 iota_subtract_fusion.pick_ref
  1.8 265.5 %fused.1 = f32[4096,256]{1,0:T(8,128)} custom-call(s32[4]{0:T(128)} %iota_subtract_fusion.pick_ref, bf16[32,2,96,256]{3,2,1,0:T(8,128)(2,1)} %spec_ref.1, s32[1,256]{1,0:T(1,128)} %order_ref.1, bf16[256,1024]{1,0:T(8,128)(2,1)} %constant.312.clone.table_ref), custom_call_target="tpu_custom_call" | custom-call | flops 16000000000 | bytes 16000000 | tf_op jit(solution)/shard_map/fused/pallas_call | solution.py:467
  267.3 0.0 copy-done
  267.3 4.2 %arrange.1 = f32[64,4,16,256]{3,2,1,0:T(8,128)} custom-call(s32[4]{0:T(128)} %copy-done, f32[4,64,16,256]{3,2,1,0:T(8,128)} %bitcast.2), custom_call_target="tpu_custom_call" | custom-call | tf_op jit(solution)/shard_map/arrange/pallas_call | solution.py:525
  (1 shorter events, 0.0 us)
Async XLA Ops:
  1.2 266.2 %copy-start = (s32[4]{0:T(128)}, s32[4]{0:T(128)S(1)}, u32[]{:S(2)}) copy-start(s32[4]{0:T(128)S(1)} %convert_reduce_fusion.place_ref) | copy-start | bytes 52
